TPU v7x, 32 devices: a whole 2x2x4 slice. The times are simulated.
32 devices in a mesh: lon: 8 (over z, x), ch: 2 (over y), lat: 2 (over core).
Axes of the slice: x: 2, y: 2, z: 4, core: 2. Of those that a mesh axis runs over, the one named last changes fastest.
Arguments:
- features: bfloat16 [40, 256, 2048], P('lat', 'lon', 'ch'), may hold values from -6 to 6
- labels: int32 [40, 256], P('lat', 'lon'), may hold values from 0 to 127
- tile_list: int32 [2, 8, 5], P('lat', 'lon'), may hold values from 0 to 5, as said below
- w_point: bfloat16 [2048, 256], P('ch'), may hold values from -0.125 to 0.125
- w_rates: bfloat16 [3, 9, 2048, 256], P(None, None, 'ch'), may hold values from -0.046875 to 0.046875
- branch_scale: float32 [4, 256], replicated, may hold values from 0.5 to 2
- branch_shift: float32 [4, 256], replicated, may hold values from -3 to 3
- w_proj: bfloat16 [1024, 256], replicated, may hold values from -0.25 to 0.25
- proj_scale: float32 [256], replicated, may hold values from 0.5 to 2
- proj_shift: float32 [256], replicated, may hold values from -3 to 3
- w_class: bfloat16 [256, 128], replicated, may hold values from -1.8 to 1.8
Outputs:
- feature_grad: bfloat16 [40, 256, 2048], P('lat', 'lon', 'ch')
Inputs may be any that keep to these rules, and one draw needn't show every extreme that they name: `tile_list`: each entry lists the distinct active tile indices of that block in increasing order, followed by padding entries equal to 5; every block has at least one active tile, some block has all 5, some block exactly one.
All inputs are finite; a program needn't handle non-finite values.
Results may differ from a plain program's by a relative error of at most 0.039.
The roundings to bfloat16 on the way count: a program that leaves them out, or rounds other values in their place, can miss the bound.
Values may be sent and summed in bfloat16 or wider, within the bound.
No kernel may reach another device: no remote copies, remote signals or barrier semaphores. Data moves between devices by JAX's collectives and lax.ppermute only.
A program may use at most 192 MiB of HBM per device.

v0:
```python
import functools

import jax
import jax.numpy as jnp
from jax import lax
from jax.experimental import pallas as pl
from jax.experimental.pallas import tpu as pltpu
from jax.sharding import PartitionSpec as P

atrous_rates = (6, 12, 18)
f32 = jnp.float32
bf16 = jnp.bfloat16
wire = jnp.float16
mebi = 1024 * 1024
groups = (((2, 0), (0, 18), 24), ((1,), (0,), 12))
halo_at = (30, 18, 0)
halo_cols = 36


def mul(lhs, rhs):
    return jnp.dot(lhs, rhs, preferred_element_type=f32)


def mul_t(lhs, rhs):
    return lax.dot_general(lhs, rhs, (((1,), (1,)), ((), ())), preferred_element_type=f32)


def call(body, kinds, out_shape, scratch, flops, moved, vmem=16):
    space = {"s": pltpu.SMEM, "v": pltpu.VMEM, "h": pltpu.HBM}
    return pl.pallas_call(
        body,
        in_specs=[pl.BlockSpec(memory_space=space[k]) for k in kinds],
        out_specs=jax.tree.map(lambda _: pl.BlockSpec(memory_space=pltpu.VMEM), out_shape),
        out_shape=out_shape,
        scratch_shapes=scratch,
        compiler_params=pltpu.CompilerParams(vmem_limit_bytes=vmem * mebi),
        cost_estimate=pl.CostEstimate(
            flops=flops // 16, bytes_accessed=moved // 16, transcendentals=0
        ),
    )


def shape(dims, kind):
    return jax.ShapeDtypeStruct(dims, kind)


def slot_of(half, halves, ch):
    return 0 if halves == 1 else (ch if half else 1 - ch)


def beside(*values):
    return values[0] if len(values) == 1 else jnp.concatenate(values, 1)


def point_kernel(halves):
    def body(place, feat, point, out, field, held, arrived):
        count = out.shape[1]
        copies = [
            pltpu.make_async_copy(feat, field, arrived.at[0]),
            pltpu.make_async_copy(point, held, arrived.at[1]),
        ]
        for copy in copies:
            copy.start()
        for copy in copies:
            copy.wait()
        total = mul(field[...], held[...])
        for half in range(halves):
            out[slot_of(half, halves, place[1])] = total[half * count : (half + 1) * count, :]

    return body


def column_steps(total, tall, taps, branch, cols_of, rows, cols):
    pixels, cut = rows * cols, atrous_rates[branch] * cols

    def row_step(u):
        start = pixels + (u - 1) * cut
        return mul(tall[start : start + pixels, :], beside(*(taps(branch, u, v) for v in cols_of)))

    total[...] = (row_step(0) + row_step(1) + row_step(2)).reshape(total.shape)


def side_taps(branches):
    return [(b, u, v) for b in branches for u in range(3) for v in (0, 2)]


def centre_taps(branches):
    return [(b, u, 1) for b in branches for u in range(3)]


def fetcher(taps, held, arrived, wanted):
    copies = [
        pltpu.make_async_copy(taps.at[tap], held.at[i], arrived.at[i])
        for i, tap in enumerate(wanted)
    ]
    for copy in copies:
        copy.start()

    def ready(branch):
        for copy, tap in zip(copies, wanted):
            if tap[0] == branch:
                copy.wait()

    return ready, lambda *tap: held[wanted.index(tap)]


def side_kernel(rows, cols, halves, branches, spots, builds):
    part, pixels = rows // halves, rows * cols
    wanted = side_taps(branches)

    def body(place, *refs):
        if builds:
            feat, other, all_taps, local_sum, halo, tall, total, held, arrived, now = refs
        else:
            tall, all_taps, local_sum, halo, total, held, arrived = refs
        lat, ch = place[0], place[1]
        width = total.shape[-1] // 2
        if builds:
            mine = pltpu.make_async_copy(feat, tall.at[pl.ds(pixels, pixels)], now)
            mine.start()
        ready, taps = fetcher(all_taps, held, arrived, wanted)
        if builds:
            spot = pl.multiple_of((1 - lat) * (2 * pixels), pixels)
            blank = pl.multiple_of(lat * (2 * pixels), pixels)
            tall[pl.ds(spot, pixels), :] = other[...]
            tall[pl.ds(blank, pixels), :] = jnp.zeros((pixels, tall.shape[1]), bf16)
            mine.wait()
        for index, (branch, at) in enumerate(zip(branches, spots)):
            rate = atrous_rates[branch]
            ready(branch)
            column_steps(total, tall, taps, branch, (0, 2), rows, cols)
            for half in range(halves):
                slot, its = slot_of(half, halves, ch), slice(half * part, (half + 1) * part)
                halo[slot, 1, :, at : at + rate, :] = total[its, cols - rate :, :width]
                halo[slot, 0, :, at : at + rate, :] = total[its, :rate, width:]
            local_sum[index, :, rate:, :] = total[:, : cols - rate, :width]
            local_sum[index, :, :rate, :] = jnp.zeros((rows, rate, width), f32)
            local_sum[index, :, : cols - rate, :] += total[:, rate:, width:]

    return body


def centre_kernel(rows, cols, halves):
    part = rows // halves

    def body(place, tall, all_taps, *refs):
        local_sums, (out, total, held, arrived) = refs[: len(groups)], refs[len(groups) :]
        order = [b for g in groups for b in g[0]]
        ready, taps = fetcher(all_taps, held, arrived, centre_taps(order))
        width = total.shape[-1]
        for number, (branches, _, _) in enumerate(groups):
            for index, branch in enumerate(branches):
                ready(branch)
                column_steps(total, tall, taps, branch, (1,), rows, cols)
                for half in range(halves):
                    its = slice(half * part, (half + 1) * part)
                    value = total[its] + local_sums[number][index, its]
                    slot = slot_of(half, halves, place[1])
                    out[slot, :, branch * width : (branch + 1) * width] = value.reshape(
                        part * cols, width
                    )

    return body


def head_kernel(rows, cols, width):
    pixels = rows * cols

    def body(
        place, own_point, came_point, own, came, left_a, right_a, left_b, right_b,
        labels, active, scale, shift, w_proj, proj_scale, proj_shift, w_class,
        d_point, d_side, to_left, to_right, total, grad,
    ):
        total[:, :, :width] = (own_point[...] + came_point[...]).reshape(rows, cols, width)
        total[:, :, width:] = (own[...] + came[...]).reshape(rows, cols, 3 * width)
        edges = ((left_a, right_a), (left_b, right_b))
        for (branches, spots, _), (left, right) in zip(groups, edges):
            for branch, at in zip(branches, spots):
                rate = atrous_rates[branch]
                lanes = slice((branch + 1) * width, (branch + 2) * width)
                total[:, :rate, lanes] += left[:, at : at + rate, :]
                total[:, cols - rate :, lanes] += right[:, at : at + rate, :]
        pre = total[...].reshape(pixels, 4 * width) * scale[...] + shift[...]
        joined = jnp.maximum(pre, 0.0).astype(bf16)
        z_pre = mul(joined, w_proj[...]) * proj_scale[...] + proj_shift[...]
        hidden = jnp.maximum(z_pre, 0.0).astype(bf16)
        logits = mul(hidden, w_class[...])
        expo = jnp.exp(logits - jnp.max(logits, axis=1, keepdims=True))
        prob = expo / jnp.sum(expo, axis=1, keepdims=True)
        ids = lax.broadcasted_iota(jnp.int32, prob.shape, 1)
        onehot = jnp.where(ids == labels[...], 1.0, 0.0)
        d_logits = (active[...] * (prob - onehot)).astype(bf16)
        d_hidden = mul_t(d_logits, w_class[...]) * proj_scale[...]
        d_z = jnp.where(z_pre > 0, d_hidden, 0.0).astype(bf16)
        d_joined = mul_t(d_z, w_proj[...]) * scale[...]
        grad[...] = jnp.where(pre > 0, d_joined, 0.0).reshape(grad.shape)
        d_point[...] = grad[:, :, :width].astype(bf16)
        d_side[...] = grad[:, :, width:].astype(bf16)
        for branch, rate in enumerate(atrous_rates):
            at, lanes = halo_at[branch], slice((branch + 1) * width, (branch + 2) * width)
            to_left[:, at : at + rate, :] = grad[:, :rate, lanes].astype(bf16)
            to_right[:, at : at + rate, :] = grad[:, cols - rate :, lanes].astype(bf16)

    return body


def spread(total, field, taps, branch, steps, begin, same_band, lat, rows, part, cols):
    rate = atrous_rates[branch]

    def add(source, target, count, u):
        weights = beside(*(taps[branch, u, v] for v in steps))
        lhs = field[pl.ds(pl.multiple_of(source * cols, cols), count * cols), :]
        product = mul_t(lhs[:, : len(steps) * weights.shape[1] // len(steps)], weights)
        total[pl.ds(target, count)] += product.reshape(count, cols, product.shape[1])

    if same_band:
        first = begin == 0
        add(0, begin, part, 1)
        inward = min(part, rows - rate)
        add(
            jnp.where(first, 0, part - inward),
            jnp.where(first, rate, rows - inward - rate),
            inward,
            jnp.where(first, 2, 0),
        )
        if part > rate:
            outward = part - rate
            add(
                jnp.where(first, rate, 0),
                jnp.where(first, 0, rows - outward),
                outward,
                jnp.where(first, 0, 2),
            )
    else:
        u = 2 * lat
        near, far = min(rate, part), rate - part
        is_near = (begin == 0) == (lat == 0) if part < rows else True

        def near_rows():
            add(lat * (part - near), (1 - lat) * (rows - rate) + lat * (rate - near), near, u)

        if part == rows:
            near_rows()
        else:
            pl.when(is_near)(near_rows)
            if far > 0:

                @pl.when(jnp.logical_not(is_near))
                def _():
                    add(lat * (part - far), (1 - lat) * (rows - rate + part), far, u)


back_order = (2, 1, 0)


def back_local_kernel(rows, cols, width, halves, mine, first):
    part = rows // halves

    def body(place, own, other, all_taps, *refs):
        total, fields, taps, arrived = refs[-4:]
        copies = [
            pltpu.make_async_copy(all_taps.at[b], taps.at[b], arrived.at[b]) for b in back_order
        ]
        for copy in copies:
            copy.start()
        lat, ch = place[0], place[1]
        begin = 0 if halves == 1 else (ch if mine else 1 - ch) * part
        total[...] = jnp.zeros_like(total) if first else refs[0][...]
        for copy, branch in zip(copies, back_order):
            rate = atrous_rates[branch]
            lanes = slice(branch * width, (branch + 1) * width)
            for source, same_band in ((own, True), (other, False)):
                field = fields.at[2 * branch + same_band]
                value = source[:, :, lanes].astype(f32)
                zeros = jnp.zeros((part, rate, width), f32)
                left = jnp.concatenate([value[:, rate:, :], zeros], 1)
                right = jnp.concatenate([zeros, value[:, : cols - rate, :]], 1)
                for step, shifted in enumerate((left, value, right)):
                    field[:, step * width : (step + 1) * width] = shifted.reshape(
                        part * cols, width
                    ).astype(bf16)
                if same_band:
                    copy.wait()
                spread(
                    total, field, taps, branch, (0, 1, 2), begin, same_band, lat, rows, part, cols
                )

    return body


def back_halo_kernel(rows, cols, width, halves, mine, last):
    part = rows // halves

    def body(place, own, other, point, all_taps, acc, out, fields, taps, arrived, *refs):
        copies = {
            (b, u, v): pltpu.make_async_copy(
                all_taps.at[b, u, v], taps.at[b, u, v], arrived.at[b, u, v]
            )
            for b in back_order
            for u in range(3)
            for v in (0, 2)
        }
        for copy in copies.values():
            copy.start()
        total = refs[0] if last else out
        total[...] = acc[...]
        lat, ch = place[0], place[1]
        begin = 0 if halves == 1 else (ch if mine else 1 - ch) * part
        block = own[:, 2 * halo_cols :, :].reshape(part * cols, width)
        product = mul_t(block, point[...])
        total[pl.ds(begin, part)] += product.reshape(part, cols, product.shape[1])
        for branch in back_order:
            rate, at = atrous_rates[branch], halo_at[branch]
            for source, same_band in ((own, True), (other, False)):
                field = fields.at[2 * branch + same_band]
                left = source[:, at : at + rate, :].astype(f32)
                right = source[:, halo_cols + at : halo_cols + at + rate, :].astype(f32)
                zeros = jnp.zeros((part, cols - rate, width), f32)
                for step, value in enumerate(
                    (jnp.concatenate([left, zeros], 1), jnp.concatenate([zeros, right], 1))
                ):
                    field[:, step * width : (step + 1) * width] = value.reshape(
                        part * cols, width
                    ).astype(bf16)
                if same_band:
                    for tap, copy in copies.items():
                        if tap[0] == branch:
                            copy.wait()
                spread(total, field, taps, branch, (2, 0), begin, same_band, lat, rows, part, cols)
        if last:
            out[...] = total[...].astype(bf16)

    return body


def shift_pairs(size, step):
    return [(i, (i + step) % size) for i in range(size)]


def after(value, *first):
    return lax.optimization_barrier((value, *first))[0]


def local(
    features, labels, tile_list, w_point, w_rates, branch_scale, branch_shift,
    w_proj, proj_scale, proj_shift, w_class,
):
    rows, cols, chans = features.shape
    pixels = rows * cols
    width = w_point.shape[1]
    lon_size, ch_size, lat_size = (lax.axis_size(a) for a in ("lon", "ch", "lat"))
    assert lat_size == 2 and max(atrous_rates) <= min(rows, cols)
    halves = 2 if ch_size == 2 else 1
    part = rows // halves
    count = pixels // halves
    lat, ch = lax.axis_index("lat"), lax.axis_index("ch")
    place = jnp.stack([lat, ch]).astype(jnp.int32)
    taps = w_rates.reshape(3, 3, 3, chans, width)
    tap_flops = 2 * pixels * chans * width
    tap_bytes = 2 * chans * width

    def swap_lat(value):
        return lax.ppermute(value, "lat", shift_pairs(2, 1))

    def swap_ch(value):
        return lax.ppermute(value, "ch", shift_pairs(2, 1))

    def to_left(value):
        return lax.ppermute(value, "lon", shift_pairs(lon_size, -1))

    def to_right(value):
        return lax.ppermute(value, "lon", shift_pairs(lon_size, 1))

    gone = []

    def reduce_ch(parts):
        if halves == 2:
            sent = parts[0].astype(wire)
            gone.append(sent)
            return parts[1], swap_ch(sent)
        own = lax.psum(parts[0], "ch")
        return own, jnp.zeros(own.shape, wire)

    feat = features.reshape(pixels, chans)
    other = swap_lat(feat)
    tall_shape = shape((3 * pixels, chans), bf16)

    main = call(
        point_kernel(halves), "shh", shape((halves, count, width), f32),
        [
            pltpu.VMEM((pixels, chans), bf16), pltpu.VMEM((chans, width), bf16),
            pltpu.SemaphoreType.DMA((2,)),
        ],
        tap_flops, tap_bytes, vmem=56,
    )(place, feat, w_point)
    own_point, came_point = reduce_ch(main)
    halos, local_sums, edges = ([None] * len(groups) for _ in range(3))

    def tap_scratch(number):
        return [pltpu.VMEM((number, chans, width), bf16), pltpu.SemaphoreType.DMA((number,))]

    def side_call(number, builds):
        branches, spots, group_cols = groups[number]
        shapes = [
            shape((len(branches), rows, cols, width), f32),
            shape((halves, 2, part, group_cols, width), f32),
        ]
        scratch = [pltpu.VMEM((rows, cols, 2 * width), f32), *tap_scratch(6 * len(branches))]
        if builds:
            shapes.append(tall_shape)
            scratch.append(pltpu.SemaphoreType.DMA)
        return call(
            side_kernel(rows, cols, halves, branches, spots, builds),
            "shvh" if builds else "svh", tuple(shapes), scratch,
            6 * len(branches) * tap_flops, 6 * len(branches) * tap_bytes, vmem=44,
        )

    local_sums[1], halo, tall = side_call(1, True)(place, feat, other, taps)
    halos[1] = reduce_ch(halo)
    came_point = after(came_point, tall)
    local_sums[0], halo = side_call(0, False)(place, after(tall, came_point, *gone), taps)
    halos[0] = reduce_ch(halo)

    def send_halo(number, *earlier):
        own, came = halos[number]
        came = after(came, *earlier)
        halo_sum = (own + came.astype(f32)).astype(wire)
        edges[number] = (to_right(halo_sum[1]), to_left(halo_sum[0]))
        return halo_sum

    sent = send_halo(1, halo)
    main = call(
        centre_kernel(rows, cols, halves), "svh" + "v" * len(groups),
        shape((halves, count, 3 * width), f32),
        [pltpu.VMEM((rows, cols, width), f32), *tap_scratch(9)],
        9 * tap_flops, 9 * tap_bytes, vmem=44,
    )(place, after(tall, sent), taps, *local_sums)
    own, came = reduce_ch(main)
    send_halo(0, main)

    pixel = jnp.arange(pixels, dtype=jnp.int32)
    labels, tile_list = lax.optimization_barrier((labels, tile_list, main))[:2]
    active = jnp.any(tile_list.reshape(1, -1) == (pixel // 128)[:, None], axis=1).astype(f32)
    first = ch * count if halves == 2 else 0
    label_part = lax.dynamic_slice(labels.reshape(pixels, 1), (first, 0), (count, 1))
    active_part = lax.dynamic_slice(active.reshape(pixels, 1), (first, 0), (count, 1))

    edge_shape = shape((part, halo_cols, width), bf16)
    head_field = pltpu.VMEM((part, cols, 4 * width), f32)
    operands = (
        own_point, came_point.astype(f32), own, came.astype(f32),
        *(e.astype(f32) for pair in edges for e in pair),
        label_part, active_part,
        branch_scale.reshape(1, -1), branch_shift.reshape(1, -1), w_proj,
        proj_scale.reshape(1, -1), proj_shift.reshape(1, -1), w_class,
    )
    d_point, d_side, edge_left, edge_right = call(
        head_kernel(part, cols, width), "s" + "v" * len(operands),
        (
            shape((part, cols, width), bf16), shape((part, cols, 3 * width), bf16),
            edge_shape, edge_shape,
        ),
        [head_field, head_field],
        2 * count * width * (8 * width + 2 * w_class.shape[1]), 32 * count * width,
    )(place, *operands)

    acc_shape = shape((rows, cols, chans), f32)
    out_shape = shape((rows, cols, chans), bf16)

    def local_taps(d, mine, acc):
        body = back_local_kernel(rows, cols, width, halves, mine, acc is None)
        operands = (d, swap_lat(d), taps) + (() if acc is None else (acc,))
        return call(
            body, "svvh" + "v" * (len(operands) - 3), acc_shape,
            [
                pltpu.VMEM((6, part * cols, 3 * width), bf16), pltpu.VMEM(taps.shape, bf16),
                pltpu.SemaphoreType.DMA((3,)),
            ],
            14 * tap_flops, 14 * tap_bytes, vmem=44,
        )(place, *operands)

    def halo_taps(halo, mine, acc, last):
        body = back_halo_kernel(rows, cols, width, halves, mine, last)
        operands = (halo, swap_lat(halo), w_point, taps, acc)
        return call(
            body, "svvvhv", out_shape if last else acc_shape,
            [
                pltpu.VMEM((6, part * cols, 2 * width), bf16), pltpu.VMEM(taps.shape, bf16),
                pltpu.SemaphoreType.DMA((3, 3, 3)),
            ]
            + [pltpu.VMEM((rows, cols, chans), f32)] * last,
            5 * tap_flops, 14 * tap_bytes, vmem=44,
        )(place, *operands)

    left, right = to_right(edge_right), to_left(edge_left)
    acc = local_taps(d_side, True, None)
    halo_mine = jnp.concatenate([after(left, acc), right, d_point], 1)
    if halves == 2:
        d_came = after(swap_ch(d_side), acc)
        halo_came = swap_ch(halo_mine)
        acc = halo_taps(halo_mine, True, acc, False)
        acc = local_taps(d_came, False, acc)
        return halo_taps(after(halo_came, acc), False, acc, True)
    return halo_taps(halo_mine, True, acc, True)


def solution(mesh):
    placed = (
        P("lat", "lon", "ch"),
        P("lat", "lon"),
        P("lat", "lon", None),
        P("ch", None),
        P(None, None, "ch", None),
        P(),
        P(),
        P(),
        P(),
        P(),
        P(),
    )
    return jax.shard_map(
        local, mesh=mesh, in_specs=placed, out_specs=P("lat", "lon", "ch"), check_vma=False
    )
```

profile of v0, /device:TPU:1, one launch (start us, length us, event | category | flops | bytes accessed | tf_op | source)
XLA Modules:
  0.0 91.1 jit_solution(7965870927505939184)
XLA Ops:
  0.1 0.7 pad_add_fusion.place
  0.7 3.6 %shard_map.109 = f32[2,320,256]{2,1,0:T(8,128)} custom-call(s32[2]{0:T(128)} %pad_add_fusion.place, bf16[640,1024]{1,0:T(8,128)(2,1)} %bitcast.42, bf16[1024,256]{1,0:T(8,128)(2,1)} %point.5), custom_call_target="tpu_custom_call" | custom-call | flops 20971520 | bytes 32768 | tf_op jit(solution)/shard_map/pallas_call | solution.py:388
  4.3 1.1 %fusion.4 = (f16[320,256]{1,0:T(8,128)(2,1)S(1)}, f32[320,256]{1,0:T(8,128)S(1)}) fusion(f32[2,320,256]{2,1,0:T(8,128)} %shard_map.109), kind=kLoop, calls=%fused_computation.13 | loop fusion | flops 81920 | bytes 1146880 | tf_op jit(solution)/shard_map/convert_element_type | solution.py:378
  5.4 2.8 %collective-permute-start = (f16[320,256]{1,0:T(8,128)(2,1)S(1)}, f16[320,256]{1,0:T(8,128)(2,1)S(1)}, u32[]{:S(2)}, u32[]{:S(2)}) collective-permute-start(f16[320,256]{1,0:T(8,128)(2,1)S(1)} %get-tuple-element.45), channel_id=1, source_target_pairs={{0,2},{2,0},{1,3},{3,1},{4,6},{6,4},{5,7},{7,5},{8,10},{10,8},{9,1... | collective-permute-start | bytes 491528 | tf_op jit(solution)/shard_map/ppermute | solution.py:366
  8.3 4.8 %shard_map.110 = (f32[1,20,32,256]{3,2,1,0:T(8,128)S(1)}, f32[2,2,10,12,256]{4,3,2,1,0:T(8,128)S(1)}, bf16[1920,1024]{1,0:T(8,128)(2,1)S(1)}) custom-call(s32[2]{0:T(128)S(1)} %copy-done.4, bf16[640,1024]{1,0:T(8,128)(2,1)S(1)} %bitcast.43, bf16[640,1024]{1,0:T(8,128)(2,1)S(1)} %collective-permute-done.1.refs_1_, bf16[3,3,3,1024,256]{4,3,2,1,0:T(8,128)(2,1)} %bitcast.48), custom_call_target="tpu_custom_call" | custom-call | flops 125829120 | bytes 196608 | tf_op jit(solution)/shard_map/pallas_call | solution.py:418
  13.1 1.0 %collective-permute-start.2 = (f16[2,10,12,256]{3,2,1,0:T(8,128)(2,1)S(1)}, f16[2,10,12,256]{3,2,1,0:T(8,128)(2,1)S(1)}, u32[]{:S(2)}, u32[]{:S(2)}) collective-permute-start(f16[2,10,12,256]{3,2,1,0:T(8,128)(2,1)S(1)} %fusion.5), channel_id=1, source_target_pairs={{0,2},{2,0},{1,3},{3,1},{4,6},{6,4},{5,7},{7,5},{8,10},{10,8},{9,1... | collective-permute-start | bytes 368648 | tf_op jit(solution)/shard_map/ppermute | solution.py:366
  14.1 7.0 %shard_map.111 = (f32[2,20,32,256]{3,2,1,0:T(8,128)S(1)}, f32[2,2,10,24,256]{4,3,2,1,0:T(8,128)S(1)}) custom-call(s32[2]{0:T(128)S(1)} %copy-done.4, bf16[1920,1024]{1,0:T(8,128)(2,1)S(1)} %get-tuple-element.30.refs_0_.tall, bf16[3,3,3,1024,256]{4,3,2,1,0:T(8,128)(2,1)} %bitcast.49), custom_call_target="tpu_custom_call" | custom-call | flops 251658240 | bytes 393216 | tf_op jit(solution)/shard_map/pallas_call | solution.py:421
  21.9 7.5 %shard_map.112 = f32[2,320,768]{2,1,0:T(8,128)S(1)} custom-call(s32[2]{0:T(128)S(1)} %copy-done.4, bf16[1920,1024]{1,0:T(8,128)(2,1)S(1)} %get-tuple-element.30.refs_0_.tall, bf16[3,3,3,1024,256]{4,3,2,1,0:T(8,128)(2,1)} %bitcast.50, f32[2,20,32,256]{3,2,1,0:T(8,128)S(1)} %get-tuple-element.31.refs_0_, f32[1,20,32,256]{3,2,1,0:T(8,128)S(1)} %get-tuple-element.32.refs_1_), custom_call_target="tpu_custom_call" | custom-call | flops 188743680 | bytes 294912 | tf_op jit(solution)/shard_map/pallas_call | solution.py:432
  29.6 1.0 %collective-permute-start.3 = (f16[320,768]{1,0:T(8,128)(2,1)S(1)}, f16[320,768]{1,0:T(8,128)(2,1)S(1)}, u32[]{:S(2)}, u32[]{:S(2)}) collective-permute-start(f16[320,768]{1,0:T(8,128)(2,1)S(1)} %get-tuple-element.43), channel_id=1, source_target_pairs={{0,2},{2,0},{1,3},{3,1},{4,6},{6,4},{5,7},{7,5},{8,10},{10,8},{9,1... | collective-permute-start | bytes 1474568 | tf_op jit(solution)/shard_map/ppermute | solution.py:366
  30.6 0.7 slice_bitcast_fusion.4
  31.4 1.3 %collective-permute-start.5 = (f16[10,24,256]{2,1,0:T(8,128)(2,1)S(1)}, f16[10,24,256]{2,1,0:T(8,128)(2,1)S(1)}, u32[]{:S(2)}, u32[]{:S(2)}) collective-permute-start(f16[10,24,256]{2,1,0:T(8,128)(2,1)S(1)} %get-tuple-element.48), channel_id=1, source_target_pairs={{0,4},{4,8},{8,12},{12,16},{16,20},{20,24},{24,28},{28,0},{1,5},{5... | collective-permute-start | bytes 368648 | tf_op jit(solution)/shard_map/ppermute | solution.py:372
  32.6 3.1 %collective-permute-start.6 = (f16[10,24,256]{2,1,0:T(8,128)(2,1)S(1)}, f16[10,24,256]{2,1,0:T(8,128)(2,1)S(1)}, u32[]{:S(2)}, u32[]{:S(2)}) collective-permute-start(f16[10,24,256]{2,1,0:T(8,128)(2,1)S(1)} %get-tuple-element.47), channel_id=1, source_target_pairs={{0,28},{4,0},{8,4},{12,8},{16,12},{20,16},{24,20},{28,24},{1,29},{... | collective-permute-start | bytes 368648 | tf_op jit(solution)/shard_map/ppermute | solution.py:369
  36.4 4.2 %collective-permute-start.8 = (f16[10,12,256]{2,1,0:T(8,128)(2,1)S(1)}, f16[10,12,256]{2,1,0:T(8,128)(2,1)S(1)}, u32[]{:S(2)}, u32[]{:S(2)}) collective-permute-start(f16[10,12,256]{2,1,0:T(8,128)(2,1)S(1)} %get-tuple-element.49), channel_id=1, source_target_pairs={{0,28},{4,0},{8,4},{12,8},{16,12},{20,16},{24,20},{28,24},{1,29},{... | collective-permute-start | bytes 184328 | tf_op jit(solution)/shard_map/ppermute | solution.py:369
  40.6 2.1 %collective-permute-done.7 = f16[10,12,256]{2,1,0:T(8,128)(2,1)S(1)} collective-permute-done((f16[10,12,256]{2,1,0:T(8,128)(2,1)}, f16[10,12,256]{2,1,0:T(8,128)(2,1)S(1)}, u32[]{:S(2)}, u32[]{:S(2)}) %collective-permute-start.7) | collective-permute-done | bytes 61472 | tf_op jit(solution)/shard_map/ppermute | solution.py:372
  43.0 2.0 %shard_map.113 = (bf16[10,32,256]{2,1,0:T(8,128)(2,1)S(1)}, bf16[10,32,768]{2,1,0:T(8,128)(2,1)S(1)}, bf16[10,36,256]{2,1,0:T(8,128)(2,1)S(1)}, bf16[10,36,256]{2,1,0:T(8,128)(2,1)S(1)}) custom-call(s32[2]{0:T(128)S(1)} %copy-done.4, f32[320,256]{1,0:T(8,128)S(1)} %get-tuple-element.46.own_point, f32[320,256]{1,0:T(8,128)S(1)} %convert_element_type.50.came_point, ...), custom_call_target="tpu_custom_call" | custom-call | flops 23592960 | bytes 163840 | tf_op jit(solution)/shard_map/pallas_call | solution.py:457
  45.0 3.1 %collective-permute-start.10 = (bf16[10,32,768]{2,1,0:T(8,128)(2,1)S(1)}, bf16[10,32,768]{2,1,0:T(8,128)(2,1)S(1)}, u32[]{:S(2)}, u32[]{:S(2)}) collective-permute-start(bf16[10,32,768]{2,1,0:T(8,128)(2,1)S(1)} %get-tuple-element.37.own), channel_id=1, source_target_pairs={{0,1},{1,0},{2,3},{3,2},{4,5},{5,4},{6,7},{7,6},{8,9},{9,8},{10,11... | collective-permute-start | bytes 1474568 | tf_op jit(solution)/shard_map/ppermute | solution.py:363
  48.3 4.2 %collective-permute-start.11 = (bf16[10,36,256]{2,1,0:T(8,128)(2,1)S(1)}, bf16[10,36,256]{2,1,0:T(8,128)(2,1)S(1)}, u32[]{:S(2)}, u32[]{:S(2)}) collective-permute-start(bf16[10,36,256]{2,1,0:T(8,128)(2,1)S(1)} %get-tuple-element.39), channel_id=1, source_target_pairs={{0,28},{4,0},{8,4},{12,8},{16,12},{20,16},{24,20},{28,24},{1,29},{... | collective-permute-start | bytes 552968 | tf_op jit(solution)/shard_map/ppermute | solution.py:369
  52.5 8.3 %shard_map.114.acc = f32[20,32,1024]{2,1,0:T(8,128)S(1)} custom-call(s32[2]{0:T(128)S(1)} %copy-done.4, bf16[10,32,768]{2,1,0:T(8,128)(2,1)S(1)} %get-tuple-element.37.own, bf16[10,32,768]{2,1,0:T(8,128)(2,1)S(1)} %collective-permute-done.10.other, bf16[3,3,3,1024,256]{4,3,2,1,0:T(8,128)(2,1)} %bitcast.51), custom_call_target="tpu_custom_call" | custom-call | flops 293601280 | bytes 458752 | tf_op jit(solution)/shard_map/pallas_call | solution.py:473
  60.9 1.9 %collective-permute-start.15 = (bf16[10,104,256]{2,1,0:T(8,128)(2,1)S(1)}, bf16[10,104,256]{2,1,0:T(8,128)(2,1)S(1)}, u32[]{:S(2)}, u32[]{:S(2)}) collective-permute-start(bf16[10,104,256]{2,1,0:T(8,128)(2,1)S(1)} %pad_maximum_fusion.own), channel_id=1, source_target_pairs={{0,1},{1,0},{2,3},{3,2},{4,5},{5,4},{6,7},{7,6},{8,9},{9,8},{10,11... | collective-permute-start | bytes 1597448 | tf_op jit(solution)/shard_map/ppermute | solution.py:363
  63.4 0.7 collective-permute-start.14
  64.3 6.6 %shard_map.115.refs_0_ = f32[20,32,1024]{2,1,0:T(8,128)S(1)} custom-call(s32[2]{0:T(128)S(1)} %copy-done.4, bf16[10,104,256]{2,1,0:T(8,128)(2,1)S(1)} %pad_maximum_fusion.own, bf16[10,104,256]{2,1,0:T(8,128)(2,1)S(1)} %collective-permute-done.15.other, bf16[1024,256]{1,0:T(8,128)(2,1)S(1)} %copy-done.1, bf16[3,3,3,1024,256]{4,3,2,1,0:T(8,128)(2,1)} %bitcast.52, ...), custom_call_target="tpu_custom_call" | custom-call | flops 104857600 | bytes 458752 | tf_op jit(solution)/shard_map/pallas_call | solution.py:485
  70.9 9.5 %shard_map.116.acc = f32[20,32,1024]{2,1,0:T(8,128)S(1)} custom-call(s32[2]{0:T(128)S(1)} %copy-done.4, bf16[10,32,768]{2,1,0:T(8,128)(2,1)S(1)} %collective-permute-done.13.own, bf16[10,32,768]{2,1,0:T(8,128)(2,1)S(1)} %collective-permute-done.14.other, bf16[3,3,3,1024,256]{4,3,2,1,0:T(8,128)(2,1)} %bitcast.53, f32[20,32,1024]{2,1,0:T(8,128)S(1)} %shard_map.115.refs_0_), custom_call_target="tpu_custom_call" | custom-call | flops 293601280 | bytes 458752 | tf_op jit(solution)/shard_map/pallas_call | solution.py:473
  80.6 1.8 %collective-permute-done.16.other = bf16[10,104,256]{2,1,0:T(8,128)(2,1)S(1)} collective-permute-done((bf16[10,104,256]{2,1,0:T(8,128)(2,1)S(1)}, bf16[10,104,256]{2,1,0:T(8,128)(2,1)S(1)}, u32[]{:S(2)}, u32[]{:S(2)}) %collective-permute-start.16) | collective-permute-done | bytes 532512 | tf_op jit(solution)/shard_map/ppermute | solution.py:363
  82.4 8.5 %shard_map.117 = bf16[20,32,1024]{2,1,0:T(8,128)(2,1)} custom-call(s32[2]{0:T(128)S(1)} %copy-done.4, bf16[10,104,256]{2,1,0:T(8,128)(2,1)S(1)} %collective-permute-done.12.own, bf16[10,104,256]{2,1,0:T(8,128)(2,1)S(1)} %collective-permute-done.16.other, bf16[1024,256]{1,0:T(8,128)(2,1)S(1)} %copy-done.1, bf16[3,3,3,1024,256]{4,3,2,1,0:T(8,128)(2,1)} %bitcast.54, ...), custom_call_target="tpu_custom_call" | custom-call | flops 104857600 | bytes 458752 | tf_op jit(solution)/shard_map/pallas_call | solution.py:485
  (66 shorter events, 3.1 us)
Async XLA Ops:
  0.0 8.2 %collective-permute-start.1 = (bf16[640,1024]{1,0:T(8,128)(2,1)}, bf16[640,1024]{1,0:T(8,128)(2,1)S(1)}, u32[]{:S(2)}, u32[]{:S(2)}) collective-permute-start(bf16[640,1024]{1,0:T(8,128)(2,1)} %bitcast.41), channel_id=1, source_target_pairs={{0,1},{1,0},{2,3},{3,2},{4,5},{5,4},{6,7},{7,6},{8,9},{9,8},{10,11... | collective-permute-start | bytes 3932168 | tf_op jit(solution)/shard_map/ppermute | solution.py:363
  0.7 7.5 %copy-start.8 = (f32[4,256]{1,0:T(4,128)S(1)}, f32[4,256]{1,0:T(4,128)}, u32[]{:S(2)}) copy-start(f32[4,256]{1,0:T(4,128)} %param.16) | copy-start | bytes 12292
  0.7 7.5 %copy-start.9 = (f32[4,256]{1,0:T(4,128)S(1)}, f32[4,256]{1,0:T(4,128)}, u32[]{:S(2)}) copy-start(f32[4,256]{1,0:T(4,128)} %param.17) | copy-start | bytes 12292
  0.7 7.5 %copy-start = (bf16[20,32,1024]{2,1,0:T(8,128)(2,1)S(1)}, bf16[20,32,1024]{2,1,0:T(8,128)(2,1)}, u32[]{:S(2)}) copy-start(bf16[20,32,1024]{2,1,0:T(8,128)(2,1)} %param.11) | copy-start | bytes 3932164
  0.7 7.5 %copy-start.4 = (s32[2]{0:T(128)S(1)}, s32[2]{0:T(128)}, u32[]{:S(2)}) copy-start(s32[2]{0:T(128)} %pad_add_fusion.place) | copy-start | bytes 28
  5.4 7.6 %collective-permute-start = (f16[320,256]{1,0:T(8,128)(2,1)S(1)}, f16[320,256]{1,0:T(8,128)(2,1)S(1)}, u32[]{:S(2)}, u32[]{:S(2)}) collective-permute-start(f16[320,256]{1,0:T(8,128)(2,1)S(1)} %get-tuple-element.45), channel_id=1, source_target_pairs={{0,2},{2,0},{1,3},{3,1},{4,6},{6,4},{5,7},{7,5},{8,10},{10,8},{9,1... | collective-permute-start | bytes 491528 | tf_op jit(solution)/shard_map/ppermute | solution.py:366
  13.1 8.7 %collective-permute-start.2 = (f16[2,10,12,256]{3,2,1,0:T(8,128)(2,1)S(1)}, f16[2,10,12,256]{3,2,1,0:T(8,128)(2,1)S(1)}, u32[]{:S(2)}, u32[]{:S(2)}) collective-permute-start(f16[2,10,12,256]{3,2,1,0:T(8,128)(2,1)S(1)} %fusion.5), channel_id=1, source_target_pairs={{0,2},{2,0},{1,3},{3,1},{4,6},{6,4},{5,7},{7,5},{8,10},{10,8},{9,1... | collective-permute-start | bytes 368648 | tf_op jit(solution)/shard_map/ppermute | solution.py:366
  21.2 10.0 %collective-permute-start.4 = (f16[2,10,24,256]{3,2,1,0:T(8,128)(2,1)S(1)}, f16[2,10,24,256]{3,2,1,0:T(8,128)(2,1)S(1)}, u32[]{:S(2)}, u32[]{:S(2)}) collective-permute-start(f16[2,10,24,256]{3,2,1,0:T(8,128)(2,1)S(1)} %fusion.3), channel_id=1, source_target_pairs={{0,2},{2,0},{1,3},{3,1},{4,6},{6,4},{5,7},{7,5},{8,10},{10,8},{9,1... | collective-permute-start | bytes 737288 | tf_op jit(solution)/shard_map/ppermute | solution.py:366
  29.6 6.2 %copy-start.10 = (s32[1,1,5]{2,1,0:T(1,128)S(1)}, s32[1,1,5]{2,1,0:T(1,128)}, u32[]{:S(2)}) copy-start(s32[1,1,5]{2,1,0:T(1,128)} %param.13) | copy-start | bytes 64
  29.6 6.3 %copy-start.7 = (s32[20,32]{1,0:T(8,128)S(1)}, s32[20,32]{1,0:T(8,128)}, u32[]{:S(2)}) copy-start(s32[20,32]{1,0:T(8,128)} %param.12) | copy-start | bytes 7684
  29.6 13.3 %collective-permute-start.3 = (f16[320,768]{1,0:T(8,128)(2,1)S(1)}, f16[320,768]{1,0:T(8,128)(2,1)S(1)}, u32[]{:S(2)}, u32[]{:S(2)}) collective-permute-start(f16[320,768]{1,0:T(8,128)(2,1)S(1)} %get-tuple-element.43), channel_id=1, source_target_pairs={{0,2},{2,0},{1,3},{3,1},{4,6},{6,4},{5,7},{7,5},{8,10},{10,8},{9,1... | collective-permute-start | bytes 1474568 | tf_op jit(solution)/shard_map/ppermute | solution.py:366
  31.4 11.4 %collective-permute-start.5 = (f16[10,24,256]{2,1,0:T(8,128)(2,1)S(1)}, f16[10,24,256]{2,1,0:T(8,128)(2,1)S(1)}, u32[]{:S(2)}, u32[]{:S(2)}) collective-permute-start(f16[10,24,256]{2,1,0:T(8,128)(2,1)S(1)} %get-tuple-element.48), channel_id=1, source_target_pairs={{0,4},{4,8},{8,12},{12,16},{16,20},{20,24},{24,28},{28,0},{1,5},{5... | collective-permute-start | bytes 368648 | tf_op jit(solution)/shard_map/ppermute | solution.py:372
  32.6 10.2 %collective-permute-start.6 = (f16[10,24,256]{2,1,0:T(8,128)(2,1)S(1)}, f16[10,24,256]{2,1,0:T(8,128)(2,1)S(1)}, u32[]{:S(2)}, u32[]{:S(2)}) collective-permute-start(f16[10,24,256]{2,1,0:T(8,128)(2,1)S(1)} %get-tuple-element.47), channel_id=1, source_target_pairs={{0,28},{4,0},{8,4},{12,8},{16,12},{20,16},{24,20},{28,24},{1,29},{... | collective-permute-start | bytes 368648 | tf_op jit(solution)/shard_map/ppermute | solution.py:369
  36.4 6.4 %collective-permute-start.7 = (f16[10,12,256]{2,1,0:T(8,128)(2,1)}, f16[10,12,256]{2,1,0:T(8,128)(2,1)S(1)}, u32[]{:S(2)}, u32[]{:S(2)}) collective-permute-start(f16[10,12,256]{2,1,0:T(8,128)(2,1)} %get-tuple-element.50), channel_id=1, source_target_pairs={{0,4},{4,8},{8,12},{12,16},{16,20},{20,24},{24,28},{28,0},{1,5},{5... | collective-permute-start | bytes 184328 | tf_op jit(solution)/shard_map/ppermute | solution.py:372
  36.4 6.3 %collective-permute-start.8 = (f16[10,12,256]{2,1,0:T(8,128)(2,1)S(1)}, f16[10,12,256]{2,1,0:T(8,128)(2,1)S(1)}, u32[]{:S(2)}, u32[]{:S(2)}) collective-permute-start(f16[10,12,256]{2,1,0:T(8,128)(2,1)S(1)} %get-tuple-element.49), channel_id=1, source_target_pairs={{0,28},{4,0},{8,4},{12,8},{16,12},{20,16},{24,20},{28,24},{1,29},{... | collective-permute-start | bytes 184328 | tf_op jit(solution)/shard_map/ppermute | solution.py:369
  45.0 7.4 %collective-permute-start.10 = (bf16[10,32,768]{2,1,0:T(8,128)(2,1)S(1)}, bf16[10,32,768]{2,1,0:T(8,128)(2,1)S(1)}, u32[]{:S(2)}, u32[]{:S(2)}) collective-permute-start(bf16[10,32,768]{2,1,0:T(8,128)(2,1)S(1)} %get-tuple-element.37.own), channel_id=1, source_target_pairs={{0,1},{1,0},{2,3},{3,2},{4,5},{5,4},{6,7},{7,6},{8,9},{9,8},{10,11... | collective-permute-start | bytes 1474568 | tf_op jit(solution)/shard_map/ppermute | solution.py:363
  48.2 15.2 %collective-permute-start.13 = (bf16[10,32,768]{2,1,0:T(8,128)(2,1)S(1)}, bf16[10,32,768]{2,1,0:T(8,128)(2,1)S(1)}, u32[]{:S(2)}, u32[]{:S(2)}) collective-permute-start(bf16[10,32,768]{2,1,0:T(8,128)(2,1)S(1)} %get-tuple-element.37.own), channel_id=1, source_target_pairs={{0,2},{2,0},{1,3},{3,1},{4,6},{6,4},{5,7},{7,5},{8,10},{10,8},{9,1... | collective-permute-start | bytes 1474568 | tf_op jit(solution)/shard_map/ppermute | solution.py:366
  48.3 12.6 %collective-permute-start.9 = (bf16[10,36,256]{2,1,0:T(8,128)(2,1)S(1)}, bf16[10,36,256]{2,1,0:T(8,128)(2,1)S(1)}, u32[]{:S(2)}, u32[]{:S(2)}) collective-permute-start(bf16[10,36,256]{2,1,0:T(8,128)(2,1)S(1)} %get-tuple-element.36), channel_id=1, source_target_pairs={{0,4},{4,8},{8,12},{12,16},{16,20},{20,24},{24,28},{28,0},{1,5},{5... | collective-permute-start | bytes 552968 | tf_op jit(solution)/shard_map/ppermute | solution.py:372
  48.3 12.6 %collective-permute-start.11 = (bf16[10,36,256]{2,1,0:T(8,128)(2,1)S(1)}, bf16[10,36,256]{2,1,0:T(8,128)(2,1)S(1)}, u32[]{:S(2)}, u32[]{:S(2)}) collective-permute-start(bf16[10,36,256]{2,1,0:T(8,128)(2,1)S(1)} %get-tuple-element.39), channel_id=1, source_target_pairs={{0,28},{4,0},{8,4},{12,8},{16,12},{20,16},{24,20},{28,24},{1,29},{... | collective-permute-start | bytes 552968 | tf_op jit(solution)/shard_map/ppermute | solution.py:369
  60.8 3.5 %copy-start.1 = (bf16[1024,256]{1,0:T(8,128)(2,1)S(1)}, bf16[1024,256]{1,0:T(8,128)(2,1)}, u32[]{:S(2)}) copy-start(bf16[1024,256]{1,0:T(8,128)(2,1)} %point.5) | copy-start | bytes 1572868
  60.9 3.4 %collective-permute-start.15 = (bf16[10,104,256]{2,1,0:T(8,128)(2,1)S(1)}, bf16[10,104,256]{2,1,0:T(8,128)(2,1)S(1)}, u32[]{:S(2)}, u32[]{:S(2)}) collective-permute-start(bf16[10,104,256]{2,1,0:T(8,128)(2,1)S(1)} %pad_maximum_fusion.own), channel_id=1, source_target_pairs={{0,1},{1,0},{2,3},{3,2},{4,5},{5,4},{6,7},{7,6},{8,9},{9,8},{10,11... | collective-permute-start | bytes 1597448 | tf_op jit(solution)/shard_map/ppermute | solution.py:363
  62.8 17.6 %collective-permute-start.12 = (bf16[10,104,256]{2,1,0:T(8,128)(2,1)S(1)}, bf16[10,104,256]{2,1,0:T(8,128)(2,1)S(1)}, u32[]{:S(2)}, u32[]{:S(2)}) collective-permute-start(bf16[10,104,256]{2,1,0:T(8,128)(2,1)S(1)} %pad_maximum_fusion.own), channel_id=1, source_target_pairs={{0,2},{2,0},{1,3},{3,1},{4,6},{6,4},{5,7},{7,5},{8,10},{10,8},{9,1... | collective-permute-start | bytes 1597448 | tf_op jit(solution)/shard_map/ppermute | solution.py:366
  63.4 7.5 %collective-permute-start.14 = (bf16[10,32,768]{2,1,0:T(8,128)(2,1)S(1)}, bf16[10,32,768]{2,1,0:T(8,128)(2,1)S(1)}, u32[]{:S(2)}, u32[]{:S(2)}) collective-permute-start(bf16[10,32,768]{2,1,0:T(8,128)(2,1)S(1)} %collective-permute-done.13.own), channel_id=1, source_target_pairs={{0,1},{1,0},{2,3},{3,2},{4,5},{5,4},{6,7},{7,6},{8,9},{9,8},{10,11... | collective-permute-start | bytes 1474568 | tf_op jit(solution)/shard_map/ppermute | solution.py:363
  80.4 2.0 %collective-permute-start.16 = (bf16[10,104,256]{2,1,0:T(8,128)(2,1)S(1)}, bf16[10,104,256]{2,1,0:T(8,128)(2,1)S(1)}, u32[]{:S(2)}, u32[]{:S(2)}) collective-permute-start(bf16[10,104,256]{2,1,0:T(8,128)(2,1)S(1)} %collective-permute-done.12.own), channel_id=1, source_target_pairs={{0,1},{1,0},{2,3},{3,2},{4,5},{5,4},{6,7},{7,6},{8,9},{9,8},{10,11... | collective-permute-start | bytes 1597448 | tf_op jit(solution)/shard_map/ppermute | solution.py:363
  (4 other events, 9.3 us)
where the time goes:
time: 91.3 us; the launch traced here: 91.1 us
  Pallas kernels  57.9 us (63%)
  starting transfers between devices  24.8 us (27%)
  waiting for transfers between devices  4.17 us (5%)
  other arithmetic  2.39 us (3%)
  local copies, waits for them, and re-layouts  1.29 us (1%)
    pallas_call x2, Pallas kernels, local_taps(): call(body, 'svvh' + 'v' * (len(operands) - 3), acc_shape, [pltpu.VMEM((6,...  17.8 us
    pallas_call x2, Pallas kernels, halo_taps(): call(body, 'svvvhv', out_shape if last else acc_shape, [pltpu.VMEM((6, pa...  15 us
    ppermute x3, starting transfers between devices, to_left(): return lax.ppermute(value, 'lon', shift_pairs(lon_size, -1))  11.5 us
    pallas_call x1, Pallas kernels, local(): call(centre_kernel(rows, cols, halves), 'svh' + 'v' * len(groups), shape(...  7.55 us
    pallas_call x1, Pallas kernels, local(): side_call(0, False)(place, after(tall, came_point, *gone), taps)  7.01 us
    ppermute x6, starting transfers between devices, swap_ch(): return lax.ppermute(value, 'ch', shift_pairs(2, 1))  6.03 us
    ppermute x5, starting transfers between devices, swap_lat(): return lax.ppermute(value, 'lat', shift_pairs(2, 1))  5.96 us
    pallas_call x1, Pallas kernels, local(): local_sums[1], halo, tall = side_call(1, True)(place, feat, other, taps)  4.81 us
  transfers between devices with their start and end apart: 17, of which 3 were waited for; matrix products, arithmetic and copies ran while one was open for 4% of the time, Pallas kernels for 52%

commit v1 on v0

--- a/solution.py
+++ b/solution.py
@@ -52,20 +52,19 @@
     return values[0] if len(values) == 1 else jnp.concatenate(values, 1)
 
 
-def point_kernel(halves):
-    def body(place, feat, point, out, field, held, arrived):
-        count = out.shape[1]
+def point_kernel():
+    def body(feat, point, taps, out, feat_held, taps_held, point_held, arrived):
         copies = [
-            pltpu.make_async_copy(feat, field, arrived.at[0]),
-            pltpu.make_async_copy(point, held, arrived.at[1]),
+            pltpu.make_async_copy(feat, feat_held, arrived.at[0]),
+            pltpu.make_async_copy(point, point_held, arrived.at[1]),
+            pltpu.make_async_copy(taps, taps_held, arrived.at[2]),
         ]
         for copy in copies:
             copy.start()
-        for copy in copies:
-            copy.wait()
-        total = mul(field[...], held[...])
-        for half in range(halves):
-            out[slot_of(half, halves, place[1])] = total[half * count : (half + 1) * count, :]
+        copies[0].wait()
+        copies[1].wait()
+        out[...] = mul(feat_held[...], point_held[...])
+        copies[2].wait()
 
     return body
 
@@ -75,59 +74,29 @@
 
     def row_step(u):
         start = pixels + (u - 1) * cut
-        return mul(tall[start : start + pixels, :], beside(*(taps(branch, u, v) for v in cols_of)))
+        return mul(tall[start : start + pixels, :], beside(*(taps[branch, u, v] for v in cols_of)))
 
     total[...] = (row_step(0) + row_step(1) + row_step(2)).reshape(total.shape)
-
-
-def side_taps(branches):
-    return [(b, u, v) for b in branches for u in range(3) for v in (0, 2)]
-
-
-def centre_taps(branches):
-    return [(b, u, 1) for b in branches for u in range(3)]
-
-
-def fetcher(taps, held, arrived, wanted):
-    copies = [
-        pltpu.make_async_copy(taps.at[tap], held.at[i], arrived.at[i])
-        for i, tap in enumerate(wanted)
-    ]
-    for copy in copies:
-        copy.start()
-
-    def ready(branch):
-        for copy, tap in zip(copies, wanted):
-            if tap[0] == branch:
-                copy.wait()
-
-    return ready, lambda *tap: held[wanted.index(tap)]
 
 
 def side_kernel(rows, cols, halves, branches, spots, builds):
     part, pixels = rows // halves, rows * cols
-    wanted = side_taps(branches)
 
     def body(place, *refs):
         if builds:
-            feat, other, all_taps, local_sum, halo, tall, total, held, arrived, now = refs
+            feat, other, taps, local_sum, halo, tall, total = refs
         else:
-            tall, all_taps, local_sum, halo, total, held, arrived = refs
+            tall, taps, local_sum, halo, total = refs
         lat, ch = place[0], place[1]
         width = total.shape[-1] // 2
         if builds:
-            mine = pltpu.make_async_copy(feat, tall.at[pl.ds(pixels, pixels)], now)
-            mine.start()
-        ready, taps = fetcher(all_taps, held, arrived, wanted)
-        if builds:
             spot = pl.multiple_of((1 - lat) * (2 * pixels), pixels)
             blank = pl.multiple_of(lat * (2 * pixels), pixels)
+            tall[pixels : 2 * pixels, :] = feat[...]
             tall[pl.ds(spot, pixels), :] = other[...]
             tall[pl.ds(blank, pixels), :] = jnp.zeros((pixels, tall.shape[1]), bf16)
-            mine.wait()
         for index, (branch, at) in enumerate(zip(branches, spots)):
             rate = atrous_rates[branch]
-            ready(branch)
             column_steps(total, tall, taps, branch, (0, 2), rows, cols)
             for half in range(halves):
                 slot, its = slot_of(half, halves, ch), slice(half * part, (half + 1) * part)
@@ -143,22 +112,22 @@
 def centre_kernel(rows, cols, halves):
     part = rows // halves
 
-    def body(place, tall, all_taps, *refs):
-        local_sums, (out, total, held, arrived) = refs[: len(groups)], refs[len(groups) :]
-        order = [b for g in groups for b in g[0]]
-        ready, taps = fetcher(all_taps, held, arrived, centre_taps(order))
+    def body(place, tall, taps, point_sum, *refs):
+        local_sums, (out, total) = refs[: len(groups)], refs[len(groups) :]
         width = total.shape[-1]
+
+        def store(value, lane):
+            for half in range(halves):
+                its = slice(half * part, (half + 1) * part)
+                out[slot_of(half, halves, place[1]), :, lane * width : (lane + 1) * width] = value(
+                    its
+                ).reshape(part * cols, width)
+
+        store(lambda its: point_sum[its.start * cols : its.stop * cols, :], 0)
         for number, (branches, _, _) in enumerate(groups):
             for index, branch in enumerate(branches):
-                ready(branch)
                 column_steps(total, tall, taps, branch, (1,), rows, cols)
-                for half in range(halves):
-                    its = slice(half * part, (half + 1) * part)
-                    value = total[its] + local_sums[number][index, its]
-                    slot = slot_of(half, halves, place[1])
-                    out[slot, :, branch * width : (branch + 1) * width] = value.reshape(
-                        part * cols, width
-                    )
+                store(lambda its: total[its] + local_sums[number][index, its], branch + 1)
 
     return body
 
@@ -167,12 +136,11 @@
     pixels = rows * cols
 
     def body(
-        place, own_point, came_point, own, came, left_a, right_a, left_b, right_b,
-        labels, active, scale, shift, w_proj, proj_scale, proj_shift, w_class,
+        place, own, came, left_a, right_a, left_b, right_b,
+        labels, active, scales, shifts, w_proj, proj_scale, proj_shift, w_class,
         d_point, d_side, to_left, to_right, total, grad,
     ):
-        total[:, :, :width] = (own_point[...] + came_point[...]).reshape(rows, cols, width)
-        total[:, :, width:] = (own[...] + came[...]).reshape(rows, cols, 3 * width)
+        total[...] = (own[...] + came[...]).reshape(total.shape)
         edges = ((left_a, right_a), (left_b, right_b))
         for (branches, spots, _), (left, right) in zip(groups, edges):
             for branch, at in zip(branches, spots):
@@ -180,7 +148,9 @@
                 lanes = slice((branch + 1) * width, (branch + 2) * width)
                 total[:, :rate, lanes] += left[:, at : at + rate, :]
                 total[:, cols - rate :, lanes] += right[:, at : at + rate, :]
-        pre = total[...].reshape(pixels, 4 * width) * scale[...] + shift[...]
+        scale = beside(*(scales[k : k + 1, :] for k in range(4)))
+        shift = beside(*(shifts[k : k + 1, :] for k in range(4)))
+        pre = total[...].reshape(pixels, 4 * width) * scale + shift
         joined = jnp.maximum(pre, 0.0).astype(bf16)
         z_pre = mul(joined, w_proj[...]) * proj_scale[...] + proj_shift[...]
         hidden = jnp.maximum(z_pre, 0.0).astype(bf16)
@@ -192,7 +162,7 @@
         d_logits = (active[...] * (prob - onehot)).astype(bf16)
         d_hidden = mul_t(d_logits, w_class[...]) * proj_scale[...]
         d_z = jnp.where(z_pre > 0, d_hidden, 0.0).astype(bf16)
-        d_joined = mul_t(d_z, w_proj[...]) * scale[...]
+        d_joined = mul_t(d_z, w_proj[...]) * scale
         grad[...] = jnp.where(pre > 0, d_joined, 0.0).reshape(grad.shape)
         d_point[...] = grad[:, :, :width].astype(bf16)
         d_side[...] = grad[:, :, width:].astype(bf16)
@@ -204,7 +174,9 @@
     return body
 
 
-def spread(total, field, taps, branch, steps, begin, same_band, lat, rows, part, cols):
+def spread(
+    total, field, taps, branch, steps, begin, same_band, lat, rows, part, cols
+):
     rate = atrous_rates[branch]
 
     def add(source, target, count, u):
@@ -256,17 +228,22 @@
 def back_local_kernel(rows, cols, width, halves, mine, first):
     part = rows // halves
 
-    def body(place, own, other, all_taps, *refs):
-        total, fields, taps, arrived = refs[-4:]
-        copies = [
-            pltpu.make_async_copy(all_taps.at[b], taps.at[b], arrived.at[b]) for b in back_order
-        ]
-        for copy in copies:
-            copy.start()
+    def body(place, own, other, taps, *refs):
+        copies = {}
+        if first:
+            all_taps, (total, taps, fields, arrived) = taps, refs
+            copies = {
+                b: pltpu.make_async_copy(all_taps.at[b], taps.at[b], arrived.at[b])
+                for b in back_order
+            }
+            for copy in copies.values():
+                copy.start()
+        else:
+            acc, total, fields = refs
         lat, ch = place[0], place[1]
         begin = 0 if halves == 1 else (ch if mine else 1 - ch) * part
-        total[...] = jnp.zeros_like(total) if first else refs[0][...]
-        for copy, branch in zip(copies, back_order):
+        total[...] = jnp.zeros_like(total) if first else acc[...]
+        for branch in back_order:
             rate = atrous_rates[branch]
             lanes = slice(branch * width, (branch + 1) * width)
             for source, same_band in ((own, True), (other, False)):
@@ -279,10 +256,11 @@
                     field[:, step * width : (step + 1) * width] = shifted.reshape(
                         part * cols, width
                     ).astype(bf16)
-                if same_band:
-                    copy.wait()
+                if first and same_band:
+                    copies[branch].wait()
                 spread(
-                    total, field, taps, branch, (0, 1, 2), begin, same_band, lat, rows, part, cols
+                    total, field, taps, branch, (0, 1, 2), begin, same_band,
+                    lat, rows, part, cols,
                 )
 
     return body
@@ -291,21 +269,11 @@
 def back_halo_kernel(rows, cols, width, halves, mine, last):
     part = rows // halves
 
-    def body(place, own, other, point, all_taps, acc, out, fields, taps, arrived, *refs):
-        copies = {
-            (b, u, v): pltpu.make_async_copy(
-                all_taps.at[b, u, v], taps.at[b, u, v], arrived.at[b, u, v]
-            )
-            for b in back_order
-            for u in range(3)
-            for v in (0, 2)
-        }
-        for copy in copies.values():
-            copy.start()
+    def body(place, own, other, taps, point, acc, out, fields, *refs):
+        lat, ch = place[0], place[1]
+        begin = 0 if halves == 1 else (ch if mine else 1 - ch) * part
         total = refs[0] if last else out
         total[...] = acc[...]
-        lat, ch = place[0], place[1]
-        begin = 0 if halves == 1 else (ch if mine else 1 - ch) * part
         block = own[:, 2 * halo_cols :, :].reshape(part * cols, width)
         product = mul_t(block, point[...])
         total[pl.ds(begin, part)] += product.reshape(part, cols, product.shape[1])
@@ -322,11 +290,10 @@
                     field[:, step * width : (step + 1) * width] = value.reshape(
                         part * cols, width
                     ).astype(bf16)
-                if same_band:
-                    for tap, copy in copies.items():
-                        if tap[0] == branch:
-                            copy.wait()
-                spread(total, field, taps, branch, (2, 0), begin, same_band, lat, rows, part, cols)
+                spread(
+                    total, field, taps, branch, (2, 0), begin, same_band,
+                    lat, rows, part, cols,
+                )
         if last:
             out[...] = total[...].astype(bf16)
 
@@ -385,19 +352,17 @@
     other = swap_lat(feat)
     tall_shape = shape((3 * pixels, chans), bf16)
 
-    main = call(
-        point_kernel(halves), "shh", shape((halves, count, width), f32),
-        [
-            pltpu.VMEM((pixels, chans), bf16), pltpu.VMEM((chans, width), bf16),
-            pltpu.SemaphoreType.DMA((2,)),
-        ],
-        tap_flops, tap_bytes, vmem=56,
-    )(place, feat, w_point)
-    own_point, came_point = reduce_ch(main)
     halos, local_sums, edges = ([None] * len(groups) for _ in range(3))
 
-    def tap_scratch(number):
-        return [pltpu.VMEM((number, chans, width), bf16), pltpu.SemaphoreType.DMA((number,))]
+    point_sum, feat_held, taps_held = call(
+        point_kernel(), "hhh",
+        (
+            shape((pixels, width), f32), shape((pixels, chans), bf16), shape(taps.shape, bf16),
+        ),
+        [pltpu.VMEM((chans, width), bf16), pltpu.SemaphoreType.DMA((3,))],
+        tap_flops, 27 * tap_bytes, vmem=36,
+    )(feat, w_point, taps)
+    other = after(other, point_sum)
 
     def side_call(number, builds):
         branches, spots, group_cols = groups[number]
@@ -405,20 +370,17 @@
             shape((len(branches), rows, cols, width), f32),
             shape((halves, 2, part, group_cols, width), f32),
         ]
-        scratch = [pltpu.VMEM((rows, cols, 2 * width), f32), *tap_scratch(6 * len(branches))]
         if builds:
             shapes.append(tall_shape)
-            scratch.append(pltpu.SemaphoreType.DMA)
         return call(
             side_kernel(rows, cols, halves, branches, spots, builds),
-            "shvh" if builds else "svh", tuple(shapes), scratch,
-            6 * len(branches) * tap_flops, 6 * len(branches) * tap_bytes, vmem=44,
+            "svvv" if builds else "svv", tuple(shapes), [pltpu.VMEM((rows, cols, 2 * width), f32)],
+            6 * len(branches) * tap_flops, 6 * len(branches) * tap_bytes,
         )
 
-    local_sums[1], halo, tall = side_call(1, True)(place, feat, other, taps)
+    local_sums[1], halo, tall = side_call(1, True)(place, feat_held, other, taps_held)
     halos[1] = reduce_ch(halo)
-    came_point = after(came_point, tall)
-    local_sums[0], halo = side_call(0, False)(place, after(tall, came_point, *gone), taps)
+    local_sums[0], halo = side_call(0, False)(place, after(tall, *gone), taps_held)
     halos[0] = reduce_ch(halo)
 
     def send_halo(number, *earlier):
@@ -430,11 +392,10 @@
 
     sent = send_halo(1, halo)
     main = call(
-        centre_kernel(rows, cols, halves), "svh" + "v" * len(groups),
-        shape((halves, count, 3 * width), f32),
-        [pltpu.VMEM((rows, cols, width), f32), *tap_scratch(9)],
-        9 * tap_flops, 9 * tap_bytes, vmem=44,
-    )(place, after(tall, sent), taps, *local_sums)
+        centre_kernel(rows, cols, halves), "svvv" + "v" * len(groups),
+        shape((halves, count, 4 * width), f32), [pltpu.VMEM((rows, cols, width), f32)],
+        10 * tap_flops, 10 * tap_bytes,
+    )(place, after(tall, sent), taps_held, point_sum, *local_sums)
     own, came = reduce_ch(main)
     send_halo(0, main)
 
@@ -448,10 +409,10 @@
     edge_shape = shape((part, halo_cols, width), bf16)
     head_field = pltpu.VMEM((part, cols, 4 * width), f32)
     operands = (
-        own_point, came_point.astype(f32), own, came.astype(f32),
+        own, came.astype(f32),
         *(e.astype(f32) for pair in edges for e in pair),
         label_part, active_part,
-        branch_scale.reshape(1, -1), branch_shift.reshape(1, -1), w_proj,
+        branch_scale, branch_shift, w_proj,
         proj_scale.reshape(1, -1), proj_shift.reshape(1, -1), w_class,
     )
     d_point, d_side, edge_left, edge_right = call(
@@ -467,39 +428,32 @@
     acc_shape = shape((rows, cols, chans), f32)
     out_shape = shape((rows, cols, chans), bf16)
 
-    def local_taps(d, mine, acc):
-        body = back_local_kernel(rows, cols, width, halves, mine, acc is None)
-        operands = (d, swap_lat(d), taps) + (() if acc is None else (acc,))
+    fields = pltpu.VMEM((6, part * cols, 3 * width), bf16)
+    acc, back_taps = call(
+        back_local_kernel(rows, cols, width, halves, True, True), "svvh",
+        (acc_shape, shape(taps.shape, bf16)), [fields, pltpu.SemaphoreType.DMA((3,))],
+        14 * tap_flops, 14 * tap_bytes, vmem=36,
+    )(place, d_side, swap_lat(d_side), taps)
+
+    def halo_taps(halo, mine, acc, last):
         return call(
-            body, "svvh" + "v" * (len(operands) - 3), acc_shape,
-            [
-                pltpu.VMEM((6, part * cols, 3 * width), bf16), pltpu.VMEM(taps.shape, bf16),
-                pltpu.SemaphoreType.DMA((3,)),
-            ],
-            14 * tap_flops, 14 * tap_bytes, vmem=44,
-        )(place, *operands)
-
-    def halo_taps(halo, mine, acc, last):
-        body = back_halo_kernel(rows, cols, width, halves, mine, last)
-        operands = (halo, swap_lat(halo), w_point, taps, acc)
-        return call(
-            body, "svvvhv", out_shape if last else acc_shape,
-            [
-                pltpu.VMEM((6, part * cols, 2 * width), bf16), pltpu.VMEM(taps.shape, bf16),
-                pltpu.SemaphoreType.DMA((3, 3, 3)),
-            ]
+            back_halo_kernel(rows, cols, width, halves, mine, last),
+            "svvvvv", out_shape if last else acc_shape,
+            [pltpu.VMEM((6, part * cols, 2 * width), bf16)]
             + [pltpu.VMEM((rows, cols, chans), f32)] * last,
-            5 * tap_flops, 14 * tap_bytes, vmem=44,
-        )(place, *operands)
+            5 * tap_flops, 14 * tap_bytes,
+        )(place, halo, swap_lat(halo), back_taps, w_point, acc)
 
     left, right = to_right(edge_right), to_left(edge_left)
-    acc = local_taps(d_side, True, None)
     halo_mine = jnp.concatenate([after(left, acc), right, d_point], 1)
     if halves == 2:
         d_came = after(swap_ch(d_side), acc)
         halo_came = swap_ch(halo_mine)
         acc = halo_taps(halo_mine, True, acc, False)
-        acc = local_taps(d_came, False, acc)
+        acc = call(
+            back_local_kernel(rows, cols, width, halves, False, False), "svvvv", acc_shape,
+            [fields], 14 * tap_flops, 14 * tap_bytes,
+        )(place, d_came, swap_lat(d_came), back_taps, acc)
         return halo_taps(after(halo_came, acc), False, acc, True)
     return halo_taps(halo_mine, True, acc, True)
 

time: 91.3 us -> 81 us (0.89)
  Pallas kernels: 57.9 us -> 45.5 us
  waiting for transfers between devices: 4.17 us -> 7.53 us
  local copies, waits for them, and re-layouts: 1.29 us -> 3.64 us
  starting transfers between devices: 24.8 us -> 23 us
  other arithmetic: 2.39 us -> 0.81 us
    pallas_call x8, Pallas kernels: 55.8 us -> 43.5 us  [the longest x2 11.1 us: halo_taps(): call(back_halo_kernel(rows, cols, width, halves, mine, last), 'svvvvv', o...]
    ppermute x6 -> x5, waiting for transfers between devices: 0.02 us -> 3.8 us  [swap_ch(): return lax.ppermute(value, 'ch', shift_pairs(2, 1))]
    unnamed x24 -> x22, local copies, waits for them, and re-layouts: 0.07 us -> 2.41 us
    ppermute x3, starting transfers between devices: 11.5 us -> 10.3 us  [to_left(): return lax.ppermute(value, 'lon', shift_pairs(lon_size, -1))]
    ppermute x3, starting transfers between devices: 1.32 us -> 2.43 us  [to_right(): return lax.ppermute(value, 'lon', shift_pairs(lon_size, 1))]
    convert_element_type x4 -> x3, other arithmetic: 1.29 us -> 0.27 us  [reduce_ch(): sent = parts[0].astype(wire)]
    ppermute x5, starting transfers between devices: 5.96 us -> 5.03 us  [swap_lat(): return lax.ppermute(value, 'lat', shift_pairs(2, 1))]
    ppermute x6 -> x5, starting transfers between devices: 6.03 us -> 5.14 us  [swap_ch(): return lax.ppermute(value, 'ch', shift_pairs(2, 1))]
  transfers between devices with their start and end apart: 17 -> 16, of which waited for: 3 -> 5; matrix products, arithmetic and copies ran while one was open for 4% -> 2% of each run, Pallas kernels for 52% -> 42%
where the time goes in v1:
time: 81 us; the launch traced here: 80.8 us
  Pallas kernels  45.5 us (56%)
  starting transfers between devices  23 us (28%)
  waiting for transfers between devices  7.53 us (9%)
  local copies, waits for them, and re-layouts  3.64 us (4%)
  other arithmetic  0.81 us (1%)
    pallas_call x2, Pallas kernels, halo_taps(): call(back_halo_kernel(rows, cols, width, halves, mine, last), 'svvvvv', o...  11.1 us
    ppermute x3, starting transfers between devices, to_left(): return lax.ppermute(value, 'lon', shift_pairs(lon_size, -1))  10.3 us
    pallas_call x1, Pallas kernels, local(): call(back_local_kernel(rows, cols, width, halves, True, True), 'svvh', (a...  8.43 us
    pallas_call x1, Pallas kernels, local(): call(back_local_kernel(rows, cols, width, halves, False, False), 'svvvv',...  6.99 us
    pallas_call x1, Pallas kernels, local(): call(point_kernel(), 'hhh', (shape((pixels, width), f32), shape((pixels,...  5.17 us
    ppermute x5, starting transfers between devices, swap_ch(): return lax.ppermute(value, 'ch', shift_pairs(2, 1))  5.14 us
    ppermute x5, starting transfers between devices, swap_lat(): return lax.ppermute(value, 'lat', shift_pairs(2, 1))  5.03 us
    pallas_call x1, Pallas kernels, local(): side_call(0, False)(place, after(tall, *gone), taps_held)  4.95 us
  transfers between devices with their start and end apart: 16, of which 5 were waited for; matrix products, arithmetic and copies ran while one was open for 2% of the time, Pallas kernels for 42%

profile of v1, /device:TPU:1, one launch (start us, length us, event | category | flops | bytes accessed | tf_op | source)
XLA Modules:
  0.0 80.8 jit_solution(5631788302623310146)
XLA Ops:
  0.1 1.0 %copy-done = bf16[1024,256]{1,0:T(8,128)(2,1)S(1)} copy-done((bf16[1024,256]{1,0:T(8,128)(2,1)S(1)}, bf16[1024,256]{1,0:T(8,128)(2,1)}, u32[]{:S(2)}) %copy-start) | copy-done | bytes 524312
  1.1 1.3 %copy-done.2 = bf16[20,32,1024]{2,1,0:T(8,128)(2,1)S(1)} copy-done((bf16[20,32,1024]{2,1,0:T(8,128)(2,1)S(1)}, bf16[20,32,1024]{2,1,0:T(8,128)(2,1)}, u32[]{:S(2)}) %copy-start.2) | copy-done | bytes 1310744
  2.4 5.2 %shard_map.109 = (f32[640,256]{1,0:T(8,128)S(1)}, bf16[640,1024]{1,0:T(8,128)(2,1)S(1)}, bf16[3,3,3,1024,256]{4,3,2,1,0:T(8,128)(2,1)S(1)}) custom-call(bf16[640,1024]{1,0:T(8,128)(2,1)S(1)} %bitcast.32, bf16[1024,256]{1,0:T(8,128)(2,1)S(1)} %copy-done, bf16[3,3,3,1024,256]{4,3,2,1,0:T(8,128)(2,1)} %bitcast.35), custom_call_target="tpu_custom_call" | custom-call | flops 20971520 | bytes 884736 | tf_op jit(solution)/shard_map/pallas_call | solution.py:357
  7.7 3.0 %shard_map.110 = (f32[1,20,32,256]{3,2,1,0:T(8,128)S(1)}, f32[2,2,10,12,256]{4,3,2,1,0:T(8,128)S(1)}, bf16[1920,1024]{1,0:T(8,128)(2,1)S(1)}) custom-call(s32[2]{0:T(128)S(1)} %pad_add_fusion.place, bf16[640,1024]{1,0:T(8,128)(2,1)S(1)} %get-tuple-element.29.refs_0_, bf16[640,1024]{1,0:T(8,128)(2,1)S(1)} %collective-permute-done.refs_1_, ...), custom_call_target="tpu_custom_call" | custom-call | flops 125829120 | bytes 196608 | tf_op jit(solution)/shard_map/pallas_call | solution.py:381
  10.7 2.8 %collective-permute-start.1 = (f16[2,10,12,256]{3,2,1,0:T(8,128)(2,1)S(1)}, f16[2,10,12,256]{3,2,1,0:T(8,128)(2,1)S(1)}, u32[]{:S(2)}, u32[]{:S(2)}) collective-permute-start(f16[2,10,12,256]{3,2,1,0:T(8,128)(2,1)S(1)} %fusion.4), channel_id=1, source_target_pairs={{0,2},{2,0},{1,3},{3,1},{4,6},{6,4},{5,7},{7,5},{8,10},{10,8},{9,1... | collective-permute-start | bytes 368648 | tf_op jit(solution)/shard_map/ppermute | solution.py:333
  13.5 5.0 %shard_map.111 = (f32[2,20,32,256]{3,2,1,0:T(8,128)S(1)}, f32[2,2,10,24,256]{4,3,2,1,0:T(8,128)S(1)}) custom-call(s32[2]{0:T(128)S(1)} %pad_add_fusion.place, bf16[1920,1024]{1,0:T(8,128)(2,1)S(1)} %get-tuple-element.38.refs_0_.tall, bf16[3,3,3,1024,256]{4,3,2,1,0:T(8,128)(2,1)S(1)} %get-tuple-element.32.refs_2_.refs_1_.taps), custom_call_target="tpu_custom_call" | custom-call | flops 251658240 | bytes 393216 | tf_op jit(solution)/shard_map/pallas_call | solution.py:383
  18.6 3.8 %shard_map.112 = f32[2,320,1024]{2,1,0:T(8,128)S(1)} custom-call(s32[2]{0:T(128)S(1)} %pad_add_fusion.place, bf16[1920,1024]{1,0:T(8,128)(2,1)S(1)} %get-tuple-element.38.refs_0_.tall, bf16[3,3,3,1024,256]{4,3,2,1,0:T(8,128)(2,1)S(1)} %get-tuple-element.32.refs_2_.refs_1_.taps, f32[640,256]{1,0:T(8,128)S(1)} %get-tuple-element.30.point_sum, ...), custom_call_target="tpu_custom_call" | custom-call | flops 209715200 | bytes 327680 | tf_op jit(solution)/shard_map/pallas_call | solution.py:394
  22.7 1.5 %collective-permute-start.2 = (f16[320,1024]{1,0:T(8,128)(2,1)S(1)}, f16[320,1024]{1,0:T(8,128)(2,1)S(1)}, u32[]{:S(2)}, u32[]{:S(2)}) collective-permute-start(f16[320,1024]{1,0:T(8,128)(2,1)S(1)} %get-tuple-element.53), channel_id=1, source_target_pairs={{0,2},{2,0},{1,3},{3,1},{4,6},{6,4},{5,7},{7,5},{8,10},{10,8},{9,1... | collective-permute-start | bytes 1966088 | tf_op jit(solution)/shard_map/ppermute | solution.py:333
  24.9 0.9 %collective-permute-done.3 = f16[2,10,24,256]{3,2,1,0:T(8,128)(2,1)S(1)} collective-permute-done((f16[2,10,24,256]{3,2,1,0:T(8,128)(2,1)S(1)}, f16[2,10,24,256]{3,2,1,0:T(8,128)(2,1)S(1)}, u32[]{:S(2)}, u32[]{:S(2)}) %collective-permute-start.3) | collective-permute-done | bytes 245792 | tf_op jit(solution)/shard_map/ppermute | solution.py:333
  25.9 1.3 %collective-permute-start.4 = (f16[10,24,256]{2,1,0:T(8,128)(2,1)S(1)}, f16[10,24,256]{2,1,0:T(8,128)(2,1)S(1)}, u32[]{:S(2)}, u32[]{:S(2)}) collective-permute-start(f16[10,24,256]{2,1,0:T(8,128)(2,1)S(1)} %get-tuple-element.56), channel_id=1, source_target_pairs={{0,4},{4,8},{8,12},{12,16},{16,20},{20,24},{24,28},{28,0},{1,5},{5... | collective-permute-start | bytes 368648 | tf_op jit(solution)/shard_map/ppermute | solution.py:339
  27.2 3.1 %collective-permute-start.5 = (f16[10,24,256]{2,1,0:T(8,128)(2,1)S(1)}, f16[10,24,256]{2,1,0:T(8,128)(2,1)S(1)}, u32[]{:S(2)}, u32[]{:S(2)}) collective-permute-start(f16[10,24,256]{2,1,0:T(8,128)(2,1)S(1)} %get-tuple-element.55), channel_id=1, source_target_pairs={{0,28},{4,0},{8,4},{12,8},{16,12},{20,16},{24,20},{28,24},{1,29},{... | collective-permute-start | bytes 368648 | tf_op jit(solution)/shard_map/ppermute | solution.py:336
  31.0 4.2 %collective-permute-start.7 = (f16[10,12,256]{2,1,0:T(8,128)(2,1)S(1)}, f16[10,12,256]{2,1,0:T(8,128)(2,1)S(1)}, u32[]{:S(2)}, u32[]{:S(2)}) collective-permute-start(f16[10,12,256]{2,1,0:T(8,128)(2,1)S(1)} %get-tuple-element.57), channel_id=1, source_target_pairs={{0,28},{4,0},{8,4},{12,8},{16,12},{20,16},{24,20},{28,24},{1,29},{... | collective-permute-start | bytes 184328 | tf_op jit(solution)/shard_map/ppermute | solution.py:336
  35.2 2.1 %collective-permute-done.6 = f16[10,12,256]{2,1,0:T(8,128)(2,1)S(1)} collective-permute-done((f16[10,12,256]{2,1,0:T(8,128)(2,1)}, f16[10,12,256]{2,1,0:T(8,128)(2,1)S(1)}, u32[]{:S(2)}, u32[]{:S(2)}) %collective-permute-start.6) | collective-permute-done | bytes 61472 | tf_op jit(solution)/shard_map/ppermute | solution.py:339
  37.5 2.4 %collective-permute-done.2 = f16[320,1024]{1,0:T(8,128)(2,1)S(1)} collective-permute-done((f16[320,1024]{1,0:T(8,128)(2,1)S(1)}, f16[320,1024]{1,0:T(8,128)(2,1)S(1)}, u32[]{:S(2)}, u32[]{:S(2)}) %collective-permute-start.2) | collective-permute-done | bytes 655392 | tf_op jit(solution)/shard_map/ppermute | solution.py:333
  40.0 2.0 %shard_map.113 = (bf16[10,32,256]{2,1,0:T(8,128)(2,1)S(1)}, bf16[10,32,768]{2,1,0:T(8,128)(2,1)S(1)}, bf16[10,36,256]{2,1,0:T(8,128)(2,1)S(1)}, bf16[10,36,256]{2,1,0:T(8,128)(2,1)S(1)}) custom-call(s32[2]{0:T(128)S(1)} %pad_add_fusion.place, f32[320,1024]{1,0:T(8,128)S(1)} %get-tuple-element.54.own, f32[320,1024]{1,0:T(8,128)S(1)} %convert_element_type.46.came, ...), custom_call_target="tpu_custom_call" | custom-call | flops 23592960 | bytes 163840 | tf_op jit(solution)/shard_map/pallas_call | solution.py:418
  42.1 1.7 %collective-permute-start.9 = (bf16[10,32,768]{2,1,0:T(8,128)(2,1)S(1)}, bf16[10,32,768]{2,1,0:T(8,128)(2,1)S(1)}, u32[]{:S(2)}, u32[]{:S(2)}) collective-permute-start(bf16[10,32,768]{2,1,0:T(8,128)(2,1)S(1)} %get-tuple-element.45.own), channel_id=1, source_target_pairs={{0,1},{1,0},{2,3},{3,2},{4,5},{5,4},{6,7},{7,6},{8,9},{9,8},{10,11... | collective-permute-start | bytes 1474568 | tf_op jit(solution)/shard_map/ppermute | solution.py:330
  43.8 1.1 %collective-permute-start.8 = (bf16[10,36,256]{2,1,0:T(8,128)(2,1)S(1)}, bf16[10,36,256]{2,1,0:T(8,128)(2,1)S(1)}, u32[]{:S(2)}, u32[]{:S(2)}) collective-permute-start(bf16[10,36,256]{2,1,0:T(8,128)(2,1)S(1)} %get-tuple-element.44), channel_id=1, source_target_pairs={{0,4},{4,8},{8,12},{12,16},{16,20},{20,24},{24,28},{28,0},{1,5},{5... | collective-permute-start | bytes 552968 | tf_op jit(solution)/shard_map/ppermute | solution.py:339
  44.9 3.1 %collective-permute-start.10 = (bf16[10,36,256]{2,1,0:T(8,128)(2,1)S(1)}, bf16[10,36,256]{2,1,0:T(8,128)(2,1)S(1)}, u32[]{:S(2)}, u32[]{:S(2)}) collective-permute-start(bf16[10,36,256]{2,1,0:T(8,128)(2,1)S(1)} %get-tuple-element.48), channel_id=1, source_target_pairs={{0,28},{4,0},{8,4},{12,8},{16,12},{20,16},{24,20},{28,24},{1,29},{... | collective-permute-start | bytes 552968 | tf_op jit(solution)/shard_map/ppermute | solution.py:336
  48.0 8.4 %shard_map.114 = (f32[20,32,1024]{2,1,0:T(8,128)S(1)}, bf16[3,3,3,1024,256]{4,3,2,1,0:T(8,128)(2,1)S(1)}) custom-call(s32[2]{0:T(128)S(1)} %pad_add_fusion.place, bf16[10,32,768]{2,1,0:T(8,128)(2,1)S(1)} %get-tuple-element.45.own, bf16[10,32,768]{2,1,0:T(8,128)(2,1)S(1)} %collective-permute-done.9.other, bf16[3,3,3,1024,256]{4,3,2,1,0:T(8,128)(2,1)} %bitcast.36), custom_call_target="tpu_custom_call" | custom-call | flops 293601280 | bytes 458752 | tf_op jit(solution)/shard_map/pallas_call | solution.py:432
  56.5 1.7 %collective-permute-start.14 = (bf16[10,104,256]{2,1,0:T(8,128)(2,1)S(1)}, bf16[10,104,256]{2,1,0:T(8,128)(2,1)S(1)}, u32[]{:S(2)}, u32[]{:S(2)}) collective-permute-start(bf16[10,104,256]{2,1,0:T(8,128)(2,1)S(1)} %pad_maximum_fusion.own), channel_id=1, source_target_pairs={{0,1},{1,0},{2,3},{3,2},{4,5},{5,4},{6,7},{7,6},{8,9},{9,8},{10,11... | collective-permute-start | bytes 1597448 | tf_op jit(solution)/shard_map/ppermute | solution.py:330
  59.8 4.6 %shard_map.115.refs_0_ = f32[20,32,1024]{2,1,0:T(8,128)S(1)} custom-call(s32[2]{0:T(128)S(1)} %pad_add_fusion.place, bf16[10,104,256]{2,1,0:T(8,128)(2,1)S(1)} %pad_maximum_fusion.own, bf16[10,104,256]{2,1,0:T(8,128)(2,1)S(1)} %collective-permute-done.14.other, bf16[3,3,3,1024,256]{4,3,2,1,0:T(8,128)(2,1)S(1)} %get-tuple-element.51.taps, ...), custom_call_target="tpu_custom_call" | custom-call | flops 104857600 | bytes 458752 | tf_op jit(solution)/shard_map/pallas_call | solution.py:439
  64.4 7.0 %shard_map.116.acc = f32[20,32,1024]{2,1,0:T(8,128)S(1)} custom-call(s32[2]{0:T(128)S(1)} %pad_add_fusion.place, bf16[10,32,768]{2,1,0:T(8,128)(2,1)S(1)} %collective-permute-done.12.own, bf16[10,32,768]{2,1,0:T(8,128)(2,1)S(1)} %collective-permute-done.13.other, bf16[3,3,3,1024,256]{4,3,2,1,0:T(8,128)(2,1)S(1)} %get-tuple-element.51.taps, ...), custom_call_target="tpu_custom_call" | custom-call | flops 293601280 | bytes 458752 | tf_op jit(solution)/shard_map/pallas_call | solution.py:453
  72.8 1.5 %collective-permute-done.15.other = bf16[10,104,256]{2,1,0:T(8,128)(2,1)S(1)} collective-permute-done((bf16[10,104,256]{2,1,0:T(8,128)(2,1)S(1)}, bf16[10,104,256]{2,1,0:T(8,128)(2,1)S(1)}, u32[]{:S(2)}, u32[]{:S(2)}) %collective-permute-start.15) | collective-permute-done | bytes 532512 | tf_op jit(solution)/shard_map/ppermute | solution.py:330
  74.3 6.5 %shard_map.117 = bf16[20,32,1024]{2,1,0:T(8,128)(2,1)} custom-call(s32[2]{0:T(128)S(1)} %pad_add_fusion.place, bf16[10,104,256]{2,1,0:T(8,128)(2,1)S(1)} %collective-permute-done.11.own, bf16[10,104,256]{2,1,0:T(8,128)(2,1)S(1)} %collective-permute-done.15.other, bf16[3,3,3,1024,256]{4,3,2,1,0:T(8,128)(2,1)S(1)} %get-tuple-element.51.taps, ...), custom_call_target="tpu_custom_call" | custom-call | flops 104857600 | bytes 458752 | tf_op jit(solution)/shard_map/pallas_call | solution.py:439
  (60 shorter events, 5.2 us)
Async XLA Ops:
  0.0 7.7 %collective-permute-start = (bf16[640,1024]{1,0:T(8,128)(2,1)}, bf16[640,1024]{1,0:T(8,128)(2,1)S(1)}, u32[]{:S(2)}, u32[]{:S(2)}) collective-permute-start(bf16[640,1024]{1,0:T(8,128)(2,1)} %bitcast.31), channel_id=1, source_target_pairs={{0,1},{1,0},{2,3},{3,2},{4,5},{5,4},{6,7},{7,6},{8,9},{9,8},{10,11... | collective-permute-start | bytes 3932168 | tf_op jit(solution)/shard_map/ppermute | solution.py:330
  10.7 7.8 %collective-permute-start.1 = (f16[2,10,12,256]{3,2,1,0:T(8,128)(2,1)S(1)}, f16[2,10,12,256]{3,2,1,0:T(8,128)(2,1)S(1)}, u32[]{:S(2)}, u32[]{:S(2)}) collective-permute-start(f16[2,10,12,256]{3,2,1,0:T(8,128)(2,1)S(1)} %fusion.4), channel_id=1, source_target_pairs={{0,2},{2,0},{1,3},{3,1},{4,6},{6,4},{5,7},{7,5},{8,10},{10,8},{9,1... | collective-permute-start | bytes 368648 | tf_op jit(solution)/shard_map/ppermute | solution.py:333
  18.5 7.3 %collective-permute-start.3 = (f16[2,10,24,256]{3,2,1,0:T(8,128)(2,1)S(1)}, f16[2,10,24,256]{3,2,1,0:T(8,128)(2,1)S(1)}, u32[]{:S(2)}, u32[]{:S(2)}) collective-permute-start(f16[2,10,24,256]{3,2,1,0:T(8,128)(2,1)S(1)} %fusion.3), channel_id=1, source_target_pairs={{0,2},{2,0},{1,3},{3,1},{4,6},{6,4},{5,7},{7,5},{8,10},{10,8},{9,1... | collective-permute-start | bytes 737288 | tf_op jit(solution)/shard_map/ppermute | solution.py:333
  22.7 7.6 %copy-start.10 = (s32[1,1,5]{2,1,0:T(1,128)S(1)}, s32[1,1,5]{2,1,0:T(1,128)}, u32[]{:S(2)}) copy-start(s32[1,1,5]{2,1,0:T(1,128)} %param.13) | copy-start | bytes 64
  22.7 7.7 %copy-start.9 = (s32[20,32]{1,0:T(8,128)S(1)}, s32[20,32]{1,0:T(8,128)}, u32[]{:S(2)}) copy-start(s32[20,32]{1,0:T(8,128)} %param.12) | copy-start | bytes 7684
  22.7 17.1 %collective-permute-start.2 = (f16[320,1024]{1,0:T(8,128)(2,1)S(1)}, f16[320,1024]{1,0:T(8,128)(2,1)S(1)}, u32[]{:S(2)}, u32[]{:S(2)}) collective-permute-start(f16[320,1024]{1,0:T(8,128)(2,1)S(1)} %get-tuple-element.53), channel_id=1, source_target_pairs={{0,2},{2,0},{1,3},{3,1},{4,6},{6,4},{5,7},{7,5},{8,10},{10,8},{9,1... | collective-permute-start | bytes 1966088 | tf_op jit(solution)/shard_map/ppermute | solution.py:333
  25.9 11.5 %collective-permute-start.4 = (f16[10,24,256]{2,1,0:T(8,128)(2,1)S(1)}, f16[10,24,256]{2,1,0:T(8,128)(2,1)S(1)}, u32[]{:S(2)}, u32[]{:S(2)}) collective-permute-start(f16[10,24,256]{2,1,0:T(8,128)(2,1)S(1)} %get-tuple-element.56), channel_id=1, source_target_pairs={{0,4},{4,8},{8,12},{12,16},{16,20},{20,24},{24,28},{28,0},{1,5},{5... | collective-permute-start | bytes 368648 | tf_op jit(solution)/shard_map/ppermute | solution.py:339
  27.2 10.2 %collective-permute-start.5 = (f16[10,24,256]{2,1,0:T(8,128)(2,1)S(1)}, f16[10,24,256]{2,1,0:T(8,128)(2,1)S(1)}, u32[]{:S(2)}, u32[]{:S(2)}) collective-permute-start(f16[10,24,256]{2,1,0:T(8,128)(2,1)S(1)} %get-tuple-element.55), channel_id=1, source_target_pairs={{0,28},{4,0},{8,4},{12,8},{16,12},{20,16},{24,20},{28,24},{1,29},{... | collective-permute-start | bytes 368648 | tf_op jit(solution)/shard_map/ppermute | solution.py:336
  30.9 6.4 %collective-permute-start.6 = (f16[10,12,256]{2,1,0:T(8,128)(2,1)}, f16[10,12,256]{2,1,0:T(8,128)(2,1)S(1)}, u32[]{:S(2)}, u32[]{:S(2)}) collective-permute-start(f16[10,12,256]{2,1,0:T(8,128)(2,1)} %get-tuple-element.58), channel_id=1, source_target_pairs={{0,4},{4,8},{8,12},{12,16},{16,20},{20,24},{24,28},{28,0},{1,5},{5... | collective-permute-start | bytes 184328 | tf_op jit(solution)/shard_map/ppermute | solution.py:339
  31.0 6.3 %collective-permute-start.7 = (f16[10,12,256]{2,1,0:T(8,128)(2,1)S(1)}, f16[10,12,256]{2,1,0:T(8,128)(2,1)S(1)}, u32[]{:S(2)}, u32[]{:S(2)}) collective-permute-start(f16[10,12,256]{2,1,0:T(8,128)(2,1)S(1)} %get-tuple-element.57), channel_id=1, source_target_pairs={{0,28},{4,0},{8,4},{12,8},{16,12},{20,16},{24,20},{28,24},{1,29},{... | collective-permute-start | bytes 184328 | tf_op jit(solution)/shard_map/ppermute | solution.py:336
  37.3 2.6 %copy-start.3 = (bf16[1024,256]{1,0:T(8,128)(2,1)S(1)}, bf16[1024,256]{1,0:T(8,128)(2,1)}, u32[]{:S(2)}) copy-start(bf16[1024,256]{1,0:T(8,128)(2,1)} %w_proj.1) | copy-start | bytes 1572868
  37.4 2.6 %copy-start.4 = (bf16[256,128]{1,0:T(8,128)(2,1)S(1)}, bf16[256,128]{1,0:T(8,128)(2,1)}, u32[]{:S(2)}) copy-start(bf16[256,128]{1,0:T(8,128)(2,1)} %w_class.1) | copy-start | bytes 196612
  37.4 2.6 %copy-start.5 = (f32[4,256]{1,0:T(4,128)S(1)}, f32[4,256]{1,0:T(4,128)}, u32[]{:S(2)}) copy-start(f32[4,256]{1,0:T(4,128)} %scales.1) | copy-start | bytes 12292
  37.4 2.6 %copy-start.6 = (f32[4,256]{1,0:T(4,128)S(1)}, f32[4,256]{1,0:T(4,128)}, u32[]{:S(2)}) copy-start(f32[4,256]{1,0:T(4,128)} %shifts.1) | copy-start | bytes 12292
  37.4 2.6 %copy-start.7 = (f32[256]{0:T(256)S(1)}, f32[256]{0:T(256)}, u32[]{:S(2)}) copy-start(f32[256]{0:T(256)} %param.19) | copy-start | bytes 3076
  42.1 5.9 %collective-permute-start.9 = (bf16[10,32,768]{2,1,0:T(8,128)(2,1)S(1)}, bf16[10,32,768]{2,1,0:T(8,128)(2,1)S(1)}, u32[]{:S(2)}, u32[]{:S(2)}) collective-permute-start(bf16[10,32,768]{2,1,0:T(8,128)(2,1)S(1)} %get-tuple-element.45.own), channel_id=1, source_target_pairs={{0,1},{1,0},{2,3},{3,2},{4,5},{5,4},{6,7},{7,6},{8,9},{9,8},{10,11... | collective-permute-start | bytes 1474568 | tf_op jit(solution)/shard_map/ppermute | solution.py:330
  43.8 15.3 %collective-permute-start.12 = (bf16[10,32,768]{2,1,0:T(8,128)(2,1)S(1)}, bf16[10,32,768]{2,1,0:T(8,128)(2,1)S(1)}, u32[]{:S(2)}, u32[]{:S(2)}) collective-permute-start(bf16[10,32,768]{2,1,0:T(8,128)(2,1)S(1)} %get-tuple-element.45.own), channel_id=1, source_target_pairs={{0,2},{2,0},{1,3},{3,1},{4,6},{6,4},{5,7},{7,5},{8,10},{10,8},{9,1... | collective-permute-start | bytes 1474568 | tf_op jit(solution)/shard_map/ppermute | solution.py:333
  43.8 12.7 %collective-permute-start.8 = (bf16[10,36,256]{2,1,0:T(8,128)(2,1)S(1)}, bf16[10,36,256]{2,1,0:T(8,128)(2,1)S(1)}, u32[]{:S(2)}, u32[]{:S(2)}) collective-permute-start(bf16[10,36,256]{2,1,0:T(8,128)(2,1)S(1)} %get-tuple-element.44), channel_id=1, source_target_pairs={{0,4},{4,8},{8,12},{12,16},{16,20},{20,24},{24,28},{28,0},{1,5},{5... | collective-permute-start | bytes 552968 | tf_op jit(solution)/shard_map/ppermute | solution.py:339
  44.9 11.6 %collective-permute-start.10 = (bf16[10,36,256]{2,1,0:T(8,128)(2,1)S(1)}, bf16[10,36,256]{2,1,0:T(8,128)(2,1)S(1)}, u32[]{:S(2)}, u32[]{:S(2)}) collective-permute-start(bf16[10,36,256]{2,1,0:T(8,128)(2,1)S(1)} %get-tuple-element.48), channel_id=1, source_target_pairs={{0,28},{4,0},{8,4},{12,8},{16,12},{20,16},{24,20},{28,24},{1,29},{... | collective-permute-start | bytes 552968 | tf_op jit(solution)/shard_map/ppermute | solution.py:336
  56.4 3.4 %copy-start.1 = (bf16[1024,256]{1,0:T(8,128)(2,1)S(1)}, bf16[1024,256]{1,0:T(8,128)(2,1)}, u32[]{:S(2)}) copy-start(bf16[1024,256]{1,0:T(8,128)(2,1)} %point.5) | copy-start | bytes 1572868
  56.5 3.3 %collective-permute-start.14 = (bf16[10,104,256]{2,1,0:T(8,128)(2,1)S(1)}, bf16[10,104,256]{2,1,0:T(8,128)(2,1)S(1)}, u32[]{:S(2)}, u32[]{:S(2)}) collective-permute-start(bf16[10,104,256]{2,1,0:T(8,128)(2,1)S(1)} %pad_maximum_fusion.own), channel_id=1, source_target_pairs={{0,1},{1,0},{2,3},{3,2},{4,5},{5,4},{6,7},{7,6},{8,9},{9,8},{10,11... | collective-permute-start | bytes 1597448 | tf_op jit(solution)/shard_map/ppermute | solution.py:330
  58.3 13.7 %collective-permute-start.11 = (bf16[10,104,256]{2,1,0:T(8,128)(2,1)S(1)}, bf16[10,104,256]{2,1,0:T(8,128)(2,1)S(1)}, u32[]{:S(2)}, u32[]{:S(2)}) collective-permute-start(bf16[10,104,256]{2,1,0:T(8,128)(2,1)S(1)} %pad_maximum_fusion.own), channel_id=1, source_target_pairs={{0,2},{2,0},{1,3},{3,1},{4,6},{6,4},{5,7},{7,5},{8,10},{10,8},{9,1... | collective-permute-start | bytes 1597448 | tf_op jit(solution)/shard_map/ppermute | solution.py:333
  59.1 5.4 %collective-permute-start.13 = (bf16[10,32,768]{2,1,0:T(8,128)(2,1)S(1)}, bf16[10,32,768]{2,1,0:T(8,128)(2,1)S(1)}, u32[]{:S(2)}, u32[]{:S(2)}) collective-permute-start(bf16[10,32,768]{2,1,0:T(8,128)(2,1)S(1)} %collective-permute-done.12.own), channel_id=1, source_target_pairs={{0,1},{1,0},{2,3},{3,2},{4,5},{5,4},{6,7},{7,6},{8,9},{9,8},{10,11... | collective-permute-start | bytes 1474568 | tf_op jit(solution)/shard_map/ppermute | solution.py:330
  71.9 2.4 %collective-permute-start.15 = (bf16[10,104,256]{2,1,0:T(8,128)(2,1)S(1)}, bf16[10,104,256]{2,1,0:T(8,128)(2,1)S(1)}, u32[]{:S(2)}, u32[]{:S(2)}) collective-permute-start(bf16[10,104,256]{2,1,0:T(8,128)(2,1)S(1)} %collective-permute-done.11.own), channel_id=1, source_target_pairs={{0,1},{1,0},{2,3},{3,2},{4,5},{5,4},{6,7},{7,6},{8,9},{9,8},{10,11... | collective-permute-start | bytes 1597448 | tf_op jit(solution)/shard_map/ppermute | solution.py:330
  (3 other events, 5.0 us)

commit v2 on v1

--- a/solution.py
+++ b/solution.py
@@ -266,7 +266,7 @@
     return body
 
 
-def back_halo_kernel(rows, cols, width, halves, mine, last):
+def back_halo_kernel(rows, cols, width, halves, mine, bands, last):
     part = rows // halves
 
     def body(place, own, other, taps, point, acc, out, fields, *refs):
@@ -274,12 +274,14 @@
         begin = 0 if halves == 1 else (ch if mine else 1 - ch) * part
         total = refs[0] if last else out
         total[...] = acc[...]
-        block = own[:, 2 * halo_cols :, :].reshape(part * cols, width)
-        product = mul_t(block, point[...])
-        total[pl.ds(begin, part)] += product.reshape(part, cols, product.shape[1])
+        if True in bands:
+            block = own[:, 2 * halo_cols :, :].reshape(part * cols, width)
+            product = mul_t(block, point[...])
+            total[pl.ds(begin, part)] += product.reshape(part, cols, product.shape[1])
         for branch in back_order:
             rate, at = atrous_rates[branch], halo_at[branch]
-            for source, same_band in ((own, True), (other, False)):
+            for same_band in bands:
+                source = own if same_band else other
                 field = fields.at[2 * branch + same_band]
                 left = source[:, at : at + rate, :].astype(f32)
                 right = source[:, halo_cols + at : halo_cols + at + rate, :].astype(f32)
@@ -435,27 +437,31 @@
         14 * tap_flops, 14 * tap_bytes, vmem=36,
     )(place, d_side, swap_lat(d_side), taps)
 
-    def halo_taps(halo, mine, acc, last):
+    def halo_taps(halo, other_halo, mine, bands, acc, last):
         return call(
-            back_halo_kernel(rows, cols, width, halves, mine, last),
+            back_halo_kernel(rows, cols, width, halves, mine, bands, last),
             "svvvvv", out_shape if last else acc_shape,
             [pltpu.VMEM((6, part * cols, 2 * width), bf16)]
             + [pltpu.VMEM((rows, cols, chans), f32)] * last,
             5 * tap_flops, 14 * tap_bytes,
-        )(place, halo, swap_lat(halo), back_taps, w_point, acc)
+        )(place, halo, other_halo, back_taps, w_point, acc)
 
     left, right = to_right(edge_right), to_left(edge_left)
     halo_mine = jnp.concatenate([after(left, acc), right, d_point], 1)
     if halves == 2:
         d_came = after(swap_ch(d_side), acc)
         halo_came = swap_ch(halo_mine)
-        acc = halo_taps(halo_mine, True, acc, False)
+        both = (True, False)
+        acc = halo_taps(halo_mine, swap_lat(halo_mine), True, both, acc, False)
         acc = call(
             back_local_kernel(rows, cols, width, halves, False, False), "svvvv", acc_shape,
             [fields], 14 * tap_flops, 14 * tap_bytes,
         )(place, d_came, swap_lat(d_came), back_taps, acc)
-        return halo_taps(after(halo_came, acc), False, acc, True)
-    return halo_taps(halo_mine, True, acc, True)
+        halo_came = after(halo_came, acc)
+        other_halo = swap_lat(halo_came)
+        acc = halo_taps(halo_came, halo_came, False, (True,), acc, False)
+        return halo_taps(halo_came, other_halo, False, (False,), acc, True)
+    return halo_taps(halo_mine, swap_lat(halo_mine), True, (True, False), acc, True)
 
 
 def solution(mesh):

time: 81 us -> 80 us (0.988)
  waiting for transfers between devices: 7.53 us -> 5.98 us
    ppermute x5, waiting for transfers between devices: 1.59 us -> 0.04 us  [swap_lat(): return lax.ppermute(value, 'lat', shift_pairs(2, 1))]
    pallas_call x2 -> x3, Pallas kernels: 11.1 us -> 11.5 us  [halo_taps(): call(back_halo_kernel(rows, cols, width, halves, mine, bands, last), 'svv...]
  transfers between devices with their start and end apart: 16 -> 16, of which waited for: 5 -> 4; matrix products, arithmetic and copies ran while one was open for 2% -> 2% of each run, Pallas kernels for 42% -> 47%
where the time goes in v2:
time: 80 us; the launch traced here: 79.7 us
  Pallas kernels  46 us (58%)
  starting transfers between devices  23 us (29%)
  waiting for transfers between devices  5.98 us (7%)
  local copies, waits for them, and re-layouts  3.64 us (5%)
  other arithmetic  0.81 us (1%)
    pallas_call x3, Pallas kernels, halo_taps(): call(back_halo_kernel(rows, cols, width, halves, mine, bands, last), 'svv...  11.5 us
    ppermute x3, starting transfers between devices, to_left(): return lax.ppermute(value, 'lon', shift_pairs(lon_size, -1))  10.3 us
    pallas_call x1, Pallas kernels, local(): call(back_local_kernel(rows, cols, width, halves, True, True), 'svvh', (a...  8.43 us
    pallas_call x1, Pallas kernels, local(): call(back_local_kernel(rows, cols, width, halves, False, False), 'svvvv',...  6.99 us
    pallas_call x1, Pallas kernels, local(): call(point_kernel(), 'hhh', (shape((pixels, width), f32), shape((pixels,...  5.17 us
    ppermute x5, starting transfers between devices, swap_ch(): return lax.ppermute(value, 'ch', shift_pairs(2, 1))  5.14 us
    ppermute x5, starting transfers between devices, swap_lat(): return lax.ppermute(value, 'lat', shift_pairs(2, 1))  5.03 us
    pallas_call x1, Pallas kernels, local(): side_call(0, False)(place, after(tall, *gone), taps_held)  4.95 us
  transfers between devices with their start and end apart: 16, of which 4 were waited for; matrix products, arithmetic and copies ran while one was open for 2% of the time, Pallas kernels for 47%

profile of v2, /device:TPU:1, one launch (start us, length us, event | category | flops | bytes accessed | tf_op | source)
XLA Modules:
  0.0 79.7 jit_solution(17134925368402700265)
XLA Ops:
  0.1 1.0 %copy-done = bf16[1024,256]{1,0:T(8,128)(2,1)S(1)} copy-done((bf16[1024,256]{1,0:T(8,128)(2,1)S(1)}, bf16[1024,256]{1,0:T(8,128)(2,1)}, u32[]{:S(2)}) %copy-start) | copy-done | bytes 524312
  1.1 1.3 %copy-done.2 = bf16[20,32,1024]{2,1,0:T(8,128)(2,1)S(1)} copy-done((bf16[20,32,1024]{2,1,0:T(8,128)(2,1)S(1)}, bf16[20,32,1024]{2,1,0:T(8,128)(2,1)}, u32[]{:S(2)}) %copy-start.2) | copy-done | bytes 1310744
  2.4 5.2 %shard_map.109 = (f32[640,256]{1,0:T(8,128)S(1)}, bf16[640,1024]{1,0:T(8,128)(2,1)S(1)}, bf16[3,3,3,1024,256]{4,3,2,1,0:T(8,128)(2,1)S(1)}) custom-call(bf16[640,1024]{1,0:T(8,128)(2,1)S(1)} %bitcast.32, bf16[1024,256]{1,0:T(8,128)(2,1)S(1)} %copy-done, bf16[3,3,3,1024,256]{4,3,2,1,0:T(8,128)(2,1)} %bitcast.35), custom_call_target="tpu_custom_call" | custom-call | flops 20971520 | bytes 884736 | tf_op jit(solution)/shard_map/pallas_call | solution.py:359
  7.7 3.0 %shard_map.110 = (f32[1,20,32,256]{3,2,1,0:T(8,128)S(1)}, f32[2,2,10,12,256]{4,3,2,1,0:T(8,128)S(1)}, bf16[1920,1024]{1,0:T(8,128)(2,1)S(1)}) custom-call(s32[2]{0:T(128)S(1)} %pad_add_fusion.place, bf16[640,1024]{1,0:T(8,128)(2,1)S(1)} %get-tuple-element.29.refs_0_, bf16[640,1024]{1,0:T(8,128)(2,1)S(1)} %collective-permute-done.refs_1_, ...), custom_call_target="tpu_custom_call" | custom-call | flops 125829120 | bytes 196608 | tf_op jit(solution)/shard_map/pallas_call | solution.py:383
  10.7 2.8 %collective-permute-start.1 = (f16[2,10,12,256]{3,2,1,0:T(8,128)(2,1)S(1)}, f16[2,10,12,256]{3,2,1,0:T(8,128)(2,1)S(1)}, u32[]{:S(2)}, u32[]{:S(2)}) collective-permute-start(f16[2,10,12,256]{3,2,1,0:T(8,128)(2,1)S(1)} %fusion.4), channel_id=1, source_target_pairs={{0,2},{2,0},{1,3},{3,1},{4,6},{6,4},{5,7},{7,5},{8,10},{10,8},{9,1... | collective-permute-start | bytes 368648 | tf_op jit(solution)/shard_map/ppermute | solution.py:335
  13.5 5.0 %shard_map.111 = (f32[2,20,32,256]{3,2,1,0:T(8,128)S(1)}, f32[2,2,10,24,256]{4,3,2,1,0:T(8,128)S(1)}) custom-call(s32[2]{0:T(128)S(1)} %pad_add_fusion.place, bf16[1920,1024]{1,0:T(8,128)(2,1)S(1)} %get-tuple-element.38.refs_0_.tall, bf16[3,3,3,1024,256]{4,3,2,1,0:T(8,128)(2,1)S(1)} %get-tuple-element.32.refs_2_.refs_1_.taps), custom_call_target="tpu_custom_call" | custom-call | flops 251658240 | bytes 393216 | tf_op jit(solution)/shard_map/pallas_call | solution.py:385
  18.6 3.8 %shard_map.112 = f32[2,320,1024]{2,1,0:T(8,128)S(1)} custom-call(s32[2]{0:T(128)S(1)} %pad_add_fusion.place, bf16[1920,1024]{1,0:T(8,128)(2,1)S(1)} %get-tuple-element.38.refs_0_.tall, bf16[3,3,3,1024,256]{4,3,2,1,0:T(8,128)(2,1)S(1)} %get-tuple-element.32.refs_2_.refs_1_.taps, f32[640,256]{1,0:T(8,128)S(1)} %get-tuple-element.30.point_sum, ...), custom_call_target="tpu_custom_call" | custom-call | flops 209715200 | bytes 327680 | tf_op jit(solution)/shard_map/pallas_call | solution.py:396
  22.7 1.5 %collective-permute-start.2 = (f16[320,1024]{1,0:T(8,128)(2,1)S(1)}, f16[320,1024]{1,0:T(8,128)(2,1)S(1)}, u32[]{:S(2)}, u32[]{:S(2)}) collective-permute-start(f16[320,1024]{1,0:T(8,128)(2,1)S(1)} %get-tuple-element.53), channel_id=1, source_target_pairs={{0,2},{2,0},{1,3},{3,1},{4,6},{6,4},{5,7},{7,5},{8,10},{10,8},{9,1... | collective-permute-start | bytes 1966088 | tf_op jit(solution)/shard_map/ppermute | solution.py:335
  24.9 0.9 %collective-permute-done.3 = f16[2,10,24,256]{3,2,1,0:T(8,128)(2,1)S(1)} collective-permute-done((f16[2,10,24,256]{3,2,1,0:T(8,128)(2,1)S(1)}, f16[2,10,24,256]{3,2,1,0:T(8,128)(2,1)S(1)}, u32[]{:S(2)}, u32[]{:S(2)}) %collective-permute-start.3) | collective-permute-done | bytes 245792 | tf_op jit(solution)/shard_map/ppermute | solution.py:335
  25.9 1.3 %collective-permute-start.4 = (f16[10,24,256]{2,1,0:T(8,128)(2,1)S(1)}, f16[10,24,256]{2,1,0:T(8,128)(2,1)S(1)}, u32[]{:S(2)}, u32[]{:S(2)}) collective-permute-start(f16[10,24,256]{2,1,0:T(8,128)(2,1)S(1)} %get-tuple-element.56), channel_id=1, source_target_pairs={{0,4},{4,8},{8,12},{12,16},{16,20},{20,24},{24,28},{28,0},{1,5},{5... | collective-permute-start | bytes 368648 | tf_op jit(solution)/shard_map/ppermute | solution.py:341
  27.2 3.1 %collective-permute-start.5 = (f16[10,24,256]{2,1,0:T(8,128)(2,1)S(1)}, f16[10,24,256]{2,1,0:T(8,128)(2,1)S(1)}, u32[]{:S(2)}, u32[]{:S(2)}) collective-permute-start(f16[10,24,256]{2,1,0:T(8,128)(2,1)S(1)} %get-tuple-element.55), channel_id=1, source_target_pairs={{0,28},{4,0},{8,4},{12,8},{16,12},{20,16},{24,20},{28,24},{1,29},{... | collective-permute-start | bytes 368648 | tf_op jit(solution)/shard_map/ppermute | solution.py:338
  31.0 4.2 %collective-permute-start.7 = (f16[10,12,256]{2,1,0:T(8,128)(2,1)S(1)}, f16[10,12,256]{2,1,0:T(8,128)(2,1)S(1)}, u32[]{:S(2)}, u32[]{:S(2)}) collective-permute-start(f16[10,12,256]{2,1,0:T(8,128)(2,1)S(1)} %get-tuple-element.57), channel_id=1, source_target_pairs={{0,28},{4,0},{8,4},{12,8},{16,12},{20,16},{24,20},{28,24},{1,29},{... | collective-permute-start | bytes 184328 | tf_op jit(solution)/shard_map/ppermute | solution.py:338
  35.2 2.1 %collective-permute-done.6 = f16[10,12,256]{2,1,0:T(8,128)(2,1)S(1)} collective-permute-done((f16[10,12,256]{2,1,0:T(8,128)(2,1)}, f16[10,12,256]{2,1,0:T(8,128)(2,1)S(1)}, u32[]{:S(2)}, u32[]{:S(2)}) %collective-permute-start.6) | collective-permute-done | bytes 61472 | tf_op jit(solution)/shard_map/ppermute | solution.py:341
  37.5 2.4 %collective-permute-done.2 = f16[320,1024]{1,0:T(8,128)(2,1)S(1)} collective-permute-done((f16[320,1024]{1,0:T(8,128)(2,1)S(1)}, f16[320,1024]{1,0:T(8,128)(2,1)S(1)}, u32[]{:S(2)}, u32[]{:S(2)}) %collective-permute-start.2) | collective-permute-done | bytes 655392 | tf_op jit(solution)/shard_map/ppermute | solution.py:335
  40.0 2.0 %shard_map.113 = (bf16[10,32,256]{2,1,0:T(8,128)(2,1)S(1)}, bf16[10,32,768]{2,1,0:T(8,128)(2,1)S(1)}, bf16[10,36,256]{2,1,0:T(8,128)(2,1)S(1)}, bf16[10,36,256]{2,1,0:T(8,128)(2,1)S(1)}) custom-call(s32[2]{0:T(128)S(1)} %pad_add_fusion.place, f32[320,1024]{1,0:T(8,128)S(1)} %get-tuple-element.54.own, f32[320,1024]{1,0:T(8,128)S(1)} %convert_element_type.46.came, ...), custom_call_target="tpu_custom_call" | custom-call | flops 23592960 | bytes 163840 | tf_op jit(solution)/shard_map/pallas_call | solution.py:420
  42.1 1.7 %collective-permute-start.9 = (bf16[10,32,768]{2,1,0:T(8,128)(2,1)S(1)}, bf16[10,32,768]{2,1,0:T(8,128)(2,1)S(1)}, u32[]{:S(2)}, u32[]{:S(2)}) collective-permute-start(bf16[10,32,768]{2,1,0:T(8,128)(2,1)S(1)} %get-tuple-element.45.own), channel_id=1, source_target_pairs={{0,1},{1,0},{2,3},{3,2},{4,5},{5,4},{6,7},{7,6},{8,9},{9,8},{10,11... | collective-permute-start | bytes 1474568 | tf_op jit(solution)/shard_map/ppermute | solution.py:332
  43.8 1.1 %collective-permute-start.8 = (bf16[10,36,256]{2,1,0:T(8,128)(2,1)S(1)}, bf16[10,36,256]{2,1,0:T(8,128)(2,1)S(1)}, u32[]{:S(2)}, u32[]{:S(2)}) collective-permute-start(bf16[10,36,256]{2,1,0:T(8,128)(2,1)S(1)} %get-tuple-element.44), channel_id=1, source_target_pairs={{0,4},{4,8},{8,12},{12,16},{16,20},{20,24},{24,28},{28,0},{1,5},{5... | collective-permute-start | bytes 552968 | tf_op jit(solution)/shard_map/ppermute | solution.py:341
  44.9 3.1 %collective-permute-start.10 = (bf16[10,36,256]{2,1,0:T(8,128)(2,1)S(1)}, bf16[10,36,256]{2,1,0:T(8,128)(2,1)S(1)}, u32[]{:S(2)}, u32[]{:S(2)}) collective-permute-start(bf16[10,36,256]{2,1,0:T(8,128)(2,1)S(1)} %get-tuple-element.48), channel_id=1, source_target_pairs={{0,28},{4,0},{8,4},{12,8},{16,12},{20,16},{24,20},{28,24},{1,29},{... | collective-permute-start | bytes 552968 | tf_op jit(solution)/shard_map/ppermute | solution.py:338
  48.0 8.4 %shard_map.114 = (f32[20,32,1024]{2,1,0:T(8,128)S(1)}, bf16[3,3,3,1024,256]{4,3,2,1,0:T(8,128)(2,1)S(1)}) custom-call(s32[2]{0:T(128)S(1)} %pad_add_fusion.place, bf16[10,32,768]{2,1,0:T(8,128)(2,1)S(1)} %get-tuple-element.45.own, bf16[10,32,768]{2,1,0:T(8,128)(2,1)S(1)} %collective-permute-done.9.other, bf16[3,3,3,1024,256]{4,3,2,1,0:T(8,128)(2,1)} %bitcast.36), custom_call_target="tpu_custom_call" | custom-call | flops 293601280 | bytes 458752 | tf_op jit(solution)/shard_map/pallas_call | solution.py:434
  56.5 1.7 %collective-permute-start.14 = (bf16[10,104,256]{2,1,0:T(8,128)(2,1)S(1)}, bf16[10,104,256]{2,1,0:T(8,128)(2,1)S(1)}, u32[]{:S(2)}, u32[]{:S(2)}) collective-permute-start(bf16[10,104,256]{2,1,0:T(8,128)(2,1)S(1)} %pad_maximum_fusion.own), channel_id=1, source_target_pairs={{0,1},{1,0},{2,3},{3,2},{4,5},{5,4},{6,7},{7,6},{8,9},{9,8},{10,11... | collective-permute-start | bytes 1597448 | tf_op jit(solution)/shard_map/ppermute | solution.py:332
  59.8 4.6 %shard_map.115.refs_0_ = f32[20,32,1024]{2,1,0:T(8,128)S(1)} custom-call(s32[2]{0:T(128)S(1)} %pad_add_fusion.place, bf16[10,104,256]{2,1,0:T(8,128)(2,1)S(1)} %pad_maximum_fusion.own, bf16[10,104,256]{2,1,0:T(8,128)(2,1)S(1)} %collective-permute-done.14.other, bf16[3,3,3,1024,256]{4,3,2,1,0:T(8,128)(2,1)S(1)} %get-tuple-element.51.taps, ...), custom_call_target="tpu_custom_call" | custom-call | flops 104857600 | bytes 458752 | tf_op jit(solution)/shard_map/pallas_call | solution.py:441
  64.4 7.0 %shard_map.116.acc = f32[20,32,1024]{2,1,0:T(8,128)S(1)} custom-call(s32[2]{0:T(128)S(1)} %pad_add_fusion.place, bf16[10,32,768]{2,1,0:T(8,128)(2,1)S(1)} %collective-permute-done.12.own, bf16[10,32,768]{2,1,0:T(8,128)(2,1)S(1)} %collective-permute-done.13.other, bf16[3,3,3,1024,256]{4,3,2,1,0:T(8,128)(2,1)S(1)} %get-tuple-element.51.taps, ...), custom_call_target="tpu_custom_call" | custom-call | flops 293601280 | bytes 458752 | tf_op jit(solution)/shard_map/pallas_call | solution.py:456
  72.8 3.3 %shard_map.117.acc = f32[20,32,1024]{2,1,0:T(8,128)S(1)} custom-call(s32[2]{0:T(128)S(1)} %pad_add_fusion.place, bf16[10,104,256]{2,1,0:T(8,128)(2,1)S(1)} %collective-permute-done.11.own.other, bf16[10,104,256]{2,1,0:T(8,128)(2,1)S(1)} %collective-permute-done.11.own.other, bf16[3,3,3,1024,256]{4,3,2,1,0:T(8,128)(2,1)S(1)} %get-tuple-element.51.taps, ...), custom_call_target="tpu_custom_call" | custom-call | flops 104857600 | bytes 458752 | tf_op jit(solution)/shard_map/pallas_call | solution.py:441
  76.1 3.6 %shard_map.118 = bf16[20,32,1024]{2,1,0:T(8,128)(2,1)} custom-call(s32[2]{0:T(128)S(1)} %pad_add_fusion.place, bf16[10,104,256]{2,1,0:T(8,128)(2,1)S(1)} %collective-permute-done.11.own.other, bf16[10,104,256]{2,1,0:T(8,128)(2,1)S(1)} %collective-permute-done.15.other, bf16[3,3,3,1024,256]{4,3,2,1,0:T(8,128)(2,1)S(1)} %get-tuple-element.51.taps, ...), custom_call_target="tpu_custom_call" | custom-call | flops 104857600 | bytes 458752 | tf_op jit(solution)/shard_map/pallas_call | solution.py:441
  (61 shorter events, 5.2 us)
Async XLA Ops:
  0.0 7.7 %collective-permute-start = (bf16[640,1024]{1,0:T(8,128)(2,1)}, bf16[640,1024]{1,0:T(8,128)(2,1)S(1)}, u32[]{:S(2)}, u32[]{:S(2)}) collective-permute-start(bf16[640,1024]{1,0:T(8,128)(2,1)} %bitcast.31), channel_id=1, source_target_pairs={{0,1},{1,0},{2,3},{3,2},{4,5},{5,4},{6,7},{7,6},{8,9},{9,8},{10,11... | collective-permute-start | bytes 3932168 | tf_op jit(solution)/shard_map/ppermute | solution.py:332
  10.7 7.8 %collective-permute-start.1 = (f16[2,10,12,256]{3,2,1,0:T(8,128)(2,1)S(1)}, f16[2,10,12,256]{3,2,1,0:T(8,128)(2,1)S(1)}, u32[]{:S(2)}, u32[]{:S(2)}) collective-permute-start(f16[2,10,12,256]{3,2,1,0:T(8,128)(2,1)S(1)} %fusion.4), channel_id=1, source_target_pairs={{0,2},{2,0},{1,3},{3,1},{4,6},{6,4},{5,7},{7,5},{8,10},{10,8},{9,1... | collective-permute-start | bytes 368648 | tf_op jit(solution)/shard_map/ppermute | solution.py:335
  18.5 7.3 %collective-permute-start.3 = (f16[2,10,24,256]{3,2,1,0:T(8,128)(2,1)S(1)}, f16[2,10,24,256]{3,2,1,0:T(8,128)(2,1)S(1)}, u32[]{:S(2)}, u32[]{:S(2)}) collective-permute-start(f16[2,10,24,256]{3,2,1,0:T(8,128)(2,1)S(1)} %fusion.3), channel_id=1, source_target_pairs={{0,2},{2,0},{1,3},{3,1},{4,6},{6,4},{5,7},{7,5},{8,10},{10,8},{9,1... | collective-permute-start | bytes 737288 | tf_op jit(solution)/shard_map/ppermute | solution.py:335
  22.7 7.6 %copy-start.10 = (s32[1,1,5]{2,1,0:T(1,128)S(1)}, s32[1,1,5]{2,1,0:T(1,128)}, u32[]{:S(2)}) copy-start(s32[1,1,5]{2,1,0:T(1,128)} %param.13) | copy-start | bytes 64
  22.7 7.7 %copy-start.9 = (s32[20,32]{1,0:T(8,128)S(1)}, s32[20,32]{1,0:T(8,128)}, u32[]{:S(2)}) copy-start(s32[20,32]{1,0:T(8,128)} %param.12) | copy-start | bytes 7684
  22.7 17.1 %collective-permute-start.2 = (f16[320,1024]{1,0:T(8,128)(2,1)S(1)}, f16[320,1024]{1,0:T(8,128)(2,1)S(1)}, u32[]{:S(2)}, u32[]{:S(2)}) collective-permute-start(f16[320,1024]{1,0:T(8,128)(2,1)S(1)} %get-tuple-element.53), channel_id=1, source_target_pairs={{0,2},{2,0},{1,3},{3,1},{4,6},{6,4},{5,7},{7,5},{8,10},{10,8},{9,1... | collective-permute-start | bytes 1966088 | tf_op jit(solution)/shard_map/ppermute | solution.py:335
  25.9 11.5 %collective-permute-start.4 = (f16[10,24,256]{2,1,0:T(8,128)(2,1)S(1)}, f16[10,24,256]{2,1,0:T(8,128)(2,1)S(1)}, u32[]{:S(2)}, u32[]{:S(2)}) collective-permute-start(f16[10,24,256]{2,1,0:T(8,128)(2,1)S(1)} %get-tuple-element.56), channel_id=1, source_target_pairs={{0,4},{4,8},{8,12},{12,16},{16,20},{20,24},{24,28},{28,0},{1,5},{5... | collective-permute-start | bytes 368648 | tf_op jit(solution)/shard_map/ppermute | solution.py:341
  27.2 10.2 %collective-permute-start.5 = (f16[10,24,256]{2,1,0:T(8,128)(2,1)S(1)}, f16[10,24,256]{2,1,0:T(8,128)(2,1)S(1)}, u32[]{:S(2)}, u32[]{:S(2)}) collective-permute-start(f16[10,24,256]{2,1,0:T(8,128)(2,1)S(1)} %get-tuple-element.55), channel_id=1, source_target_pairs={{0,28},{4,0},{8,4},{12,8},{16,12},{20,16},{24,20},{28,24},{1,29},{... | collective-permute-start | bytes 368648 | tf_op jit(solution)/shard_map/ppermute | solution.py:338
  30.9 6.4 %collective-permute-start.6 = (f16[10,12,256]{2,1,0:T(8,128)(2,1)}, f16[10,12,256]{2,1,0:T(8,128)(2,1)S(1)}, u32[]{:S(2)}, u32[]{:S(2)}) collective-permute-start(f16[10,12,256]{2,1,0:T(8,128)(2,1)} %get-tuple-element.58), channel_id=1, source_target_pairs={{0,4},{4,8},{8,12},{12,16},{16,20},{20,24},{24,28},{28,0},{1,5},{5... | collective-permute-start | bytes 184328 | tf_op jit(solution)/shard_map/ppermute | solution.py:341
  31.0 6.3 %collective-permute-start.7 = (f16[10,12,256]{2,1,0:T(8,128)(2,1)S(1)}, f16[10,12,256]{2,1,0:T(8,128)(2,1)S(1)}, u32[]{:S(2)}, u32[]{:S(2)}) collective-permute-start(f16[10,12,256]{2,1,0:T(8,128)(2,1)S(1)} %get-tuple-element.57), channel_id=1, source_target_pairs={{0,28},{4,0},{8,4},{12,8},{16,12},{20,16},{24,20},{28,24},{1,29},{... | collective-permute-start | bytes 184328 | tf_op jit(solution)/shard_map/ppermute | solution.py:338
  37.3 2.6 %copy-start.3 = (bf16[1024,256]{1,0:T(8,128)(2,1)S(1)}, bf16[1024,256]{1,0:T(8,128)(2,1)}, u32[]{:S(2)}) copy-start(bf16[1024,256]{1,0:T(8,128)(2,1)} %w_proj.1) | copy-start | bytes 1572868
  37.4 2.6 %copy-start.4 = (bf16[256,128]{1,0:T(8,128)(2,1)S(1)}, bf16[256,128]{1,0:T(8,128)(2,1)}, u32[]{:S(2)}) copy-start(bf16[256,128]{1,0:T(8,128)(2,1)} %w_class.1) | copy-start | bytes 196612
  37.4 2.6 %copy-start.5 = (f32[4,256]{1,0:T(4,128)S(1)}, f32[4,256]{1,0:T(4,128)}, u32[]{:S(2)}) copy-start(f32[4,256]{1,0:T(4,128)} %scales.1) | copy-start | bytes 12292
  37.4 2.6 %copy-start.6 = (f32[4,256]{1,0:T(4,128)S(1)}, f32[4,256]{1,0:T(4,128)}, u32[]{:S(2)}) copy-start(f32[4,256]{1,0:T(4,128)} %shifts.1) | copy-start | bytes 12292
  37.4 2.6 %copy-start.7 = (f32[256]{0:T(256)S(1)}, f32[256]{0:T(256)}, u32[]{:S(2)}) copy-start(f32[256]{0:T(256)} %param.19) | copy-start | bytes 3076
  42.1 5.9 %collective-permute-start.9 = (bf16[10,32,768]{2,1,0:T(8,128)(2,1)S(1)}, bf16[10,32,768]{2,1,0:T(8,128)(2,1)S(1)}, u32[]{:S(2)}, u32[]{:S(2)}) collective-permute-start(bf16[10,32,768]{2,1,0:T(8,128)(2,1)S(1)} %get-tuple-element.45.own), channel_id=1, source_target_pairs={{0,1},{1,0},{2,3},{3,2},{4,5},{5,4},{6,7},{7,6},{8,9},{9,8},{10,11... | collective-permute-start | bytes 1474568 | tf_op jit(solution)/shard_map/ppermute | solution.py:332
  43.8 15.3 %collective-permute-start.12 = (bf16[10,32,768]{2,1,0:T(8,128)(2,1)S(1)}, bf16[10,32,768]{2,1,0:T(8,128)(2,1)S(1)}, u32[]{:S(2)}, u32[]{:S(2)}) collective-permute-start(bf16[10,32,768]{2,1,0:T(8,128)(2,1)S(1)} %get-tuple-element.45.own), channel_id=1, source_target_pairs={{0,2},{2,0},{1,3},{3,1},{4,6},{6,4},{5,7},{7,5},{8,10},{10,8},{9,1... | collective-permute-start | bytes 1474568 | tf_op jit(solution)/shard_map/ppermute | solution.py:335
  43.8 12.7 %collective-permute-start.8 = (bf16[10,36,256]{2,1,0:T(8,128)(2,1)S(1)}, bf16[10,36,256]{2,1,0:T(8,128)(2,1)S(1)}, u32[]{:S(2)}, u32[]{:S(2)}) collective-permute-start(bf16[10,36,256]{2,1,0:T(8,128)(2,1)S(1)} %get-tuple-element.44), channel_id=1, source_target_pairs={{0,4},{4,8},{8,12},{12,16},{16,20},{20,24},{24,28},{28,0},{1,5},{5... | collective-permute-start | bytes 552968 | tf_op jit(solution)/shard_map/ppermute | solution.py:341
  44.9 11.6 %collective-permute-start.10 = (bf16[10,36,256]{2,1,0:T(8,128)(2,1)S(1)}, bf16[10,36,256]{2,1,0:T(8,128)(2,1)S(1)}, u32[]{:S(2)}, u32[]{:S(2)}) collective-permute-start(bf16[10,36,256]{2,1,0:T(8,128)(2,1)S(1)} %get-tuple-element.48), channel_id=1, source_target_pairs={{0,28},{4,0},{8,4},{12,8},{16,12},{20,16},{24,20},{28,24},{1,29},{... | collective-permute-start | bytes 552968 | tf_op jit(solution)/shard_map/ppermute | solution.py:338
  56.4 3.4 %copy-start.1 = (bf16[1024,256]{1,0:T(8,128)(2,1)S(1)}, bf16[1024,256]{1,0:T(8,128)(2,1)}, u32[]{:S(2)}) copy-start(bf16[1024,256]{1,0:T(8,128)(2,1)} %point.7) | copy-start | bytes 1572868
  56.5 3.3 %collective-permute-start.14 = (bf16[10,104,256]{2,1,0:T(8,128)(2,1)S(1)}, bf16[10,104,256]{2,1,0:T(8,128)(2,1)S(1)}, u32[]{:S(2)}, u32[]{:S(2)}) collective-permute-start(bf16[10,104,256]{2,1,0:T(8,128)(2,1)S(1)} %pad_maximum_fusion.own), channel_id=1, source_target_pairs={{0,1},{1,0},{2,3},{3,2},{4,5},{5,4},{6,7},{7,6},{8,9},{9,8},{10,11... | collective-permute-start | bytes 1597448 | tf_op jit(solution)/shard_map/ppermute | solution.py:332
  58.3 13.7 %collective-permute-start.11 = (bf16[10,104,256]{2,1,0:T(8,128)(2,1)S(1)}, bf16[10,104,256]{2,1,0:T(8,128)(2,1)S(1)}, u32[]{:S(2)}, u32[]{:S(2)}) collective-permute-start(bf16[10,104,256]{2,1,0:T(8,128)(2,1)S(1)} %pad_maximum_fusion.own), channel_id=1, source_target_pairs={{0,2},{2,0},{1,3},{3,1},{4,6},{6,4},{5,7},{7,5},{8,10},{10,8},{9,1... | collective-permute-start | bytes 1597448 | tf_op jit(solution)/shard_map/ppermute | solution.py:335
  59.1 5.4 %collective-permute-start.13 = (bf16[10,32,768]{2,1,0:T(8,128)(2,1)S(1)}, bf16[10,32,768]{2,1,0:T(8,128)(2,1)S(1)}, u32[]{:S(2)}, u32[]{:S(2)}) collective-permute-start(bf16[10,32,768]{2,1,0:T(8,128)(2,1)S(1)} %collective-permute-done.12.own), channel_id=1, source_target_pairs={{0,1},{1,0},{2,3},{3,2},{4,5},{5,4},{6,7},{7,6},{8,9},{9,8},{10,11... | collective-permute-start | bytes 1474568 | tf_op jit(solution)/shard_map/ppermute | solution.py:332
  71.9 4.2 %collective-permute-start.15 = (bf16[10,104,256]{2,1,0:T(8,128)(2,1)S(1)}, bf16[10,104,256]{2,1,0:T(8,128)(2,1)S(1)}, u32[]{:S(2)}, u32[]{:S(2)}) collective-permute-start(bf16[10,104,256]{2,1,0:T(8,128)(2,1)S(1)} %collective-permute-done.11.own.other), channel_id=1, source_target_pairs={{0,1},{1,0},{2,3},{3,2},{4,5},{5,4},{6,7},{7,6},{8,9},{9,8},{10,11... | collective-permute-start | bytes 1597448 | tf_op jit(solution)/shard_map/ppermute | solution.py:332
  (3 other events, 5.0 us)

commit v3 on v2

--- a/solution.py
+++ b/solution.py
@@ -136,11 +136,11 @@
     pixels = rows * cols
 
     def body(
-        place, own, came, left_a, right_a, left_b, right_b,
+        place, sums, left_a, right_a, left_b, right_b,
         labels, active, scales, shifts, w_proj, proj_scale, proj_shift, w_class,
         d_point, d_side, to_left, to_right, total, grad,
     ):
-        total[...] = (own[...] + came[...]).reshape(total.shape)
+        total[...] = sums[...].reshape(total.shape)
         edges = ((left_a, right_a), (left_b, right_b))
         for (branches, spots, _), (left, right) in zip(groups, edges):
             for branch, at in zip(branches, spots):
@@ -411,7 +411,7 @@
     edge_shape = shape((part, halo_cols, width), bf16)
     head_field = pltpu.VMEM((part, cols, 4 * width), f32)
     operands = (
-        own, came.astype(f32),
+        own + came.astype(f32),
         *(e.astype(f32) for pair in edges for e in pair),
         label_part, active_part,
         branch_scale, branch_shift, w_proj,

time: 80 us -> 82.2 us (1.028)
  other arithmetic: 0.81 us -> 2.77 us
  waiting for transfers between devices: 5.98 us -> 6.95 us
    add x0 -> x1, other arithmetic: none -> 1.34 us  [local(): own + came.astype(f32)]
    ppermute x5, waiting for transfers between devices: 0.04 us -> 1.36 us  [swap_lat(): return lax.ppermute(value, 'lat', shift_pairs(2, 1))]
    ppermute x5, starting transfers between devices: 5.03 us -> 3.85 us  [swap_lat(): return lax.ppermute(value, 'lat', shift_pairs(2, 1))]
  transfers between devices with their start and end apart: 16 -> 16, of which waited for: 4 -> 5; matrix products, arithmetic and copies ran while one was open for 2% -> 3% of each run, Pallas kernels for 47% -> 46%
where the time goes in v3:
time: 82.2 us; the launch traced here: 81.9 us
  Pallas kernels  46 us (56%)
  starting transfers between devices  22.2 us (27%)
  waiting for transfers between devices  6.95 us (8%)
  local copies, waits for them, and re-layouts  3.63 us (4%)
  other arithmetic  2.77 us (3%)
    pallas_call x3, Pallas kernels, halo_taps(): call(back_halo_kernel(rows, cols, width, halves, mine, bands, last), 'svv...  11.5 us
    ppermute x3, starting transfers between devices, to_left(): return lax.ppermute(value, 'lon', shift_pairs(lon_size, -1))  10.3 us
    pallas_call x1, Pallas kernels, local(): call(back_local_kernel(rows, cols, width, halves, True, True), 'svvh', (a...  8.43 us
    pallas_call x1, Pallas kernels, local(): call(back_local_kernel(rows, cols, width, halves, False, False), 'svvvv',...  6.99 us
    ppermute x5, starting transfers between devices, swap_ch(): return lax.ppermute(value, 'ch', shift_pairs(2, 1))  5.55 us
    pallas_call x1, Pallas kernels, local(): call(point_kernel(), 'hhh', (shape((pixels, width), f32), shape((pixels,...  5.17 us
    pallas_call x1, Pallas kernels, local(): side_call(0, False)(place, after(tall, *gone), taps_held)  4.95 us
    ppermute x5, starting transfers between devices, swap_lat(): return lax.ppermute(value, 'lat', shift_pairs(2, 1))  3.85 us
  transfers between devices with their start and end apart: 16, of which 5 were waited for; matrix products, arithmetic and copies ran while one was open for 3% of the time, Pallas kernels for 46%

profile of v3, /device:TPU:1, one launch (start us, length us, event | category | flops | bytes accessed | tf_op | source)
XLA Modules:
  0.0 81.9 jit_solution(13925942792160283974)
XLA Ops:
  1.1 1.3 %copy-done.2 = bf16[20,32,1024]{2,1,0:T(8,128)(2,1)S(1)} copy-done((bf16[20,32,1024]{2,1,0:T(8,128)(2,1)S(1)}, bf16[20,32,1024]{2,1,0:T(8,128)(2,1)}, u32[]{:S(2)}) %copy-start.2) | copy-done | bytes 1310744
  2.4 5.2 %shard_map.109 = (f32[640,256]{1,0:T(8,128)S(1)}, bf16[640,1024]{1,0:T(8,128)(2,1)S(1)}, bf16[3,3,3,1024,256]{4,3,2,1,0:T(8,128)(2,1)S(1)}) custom-call(bf16[640,1024]{1,0:T(8,128)(2,1)S(1)} %bitcast.34, bf16[1024,256]{1,0:T(8,128)(2,1)S(1)} %copy-done, bf16[3,3,3,1024,256]{4,3,2,1,0:T(8,128)(2,1)} %bitcast.37), custom_call_target="tpu_custom_call" | custom-call | flops 20971520 | bytes 884736 | tf_op jit(solution)/shard_map/pallas_call | solution.py:359
  7.7 3.0 %shard_map.110 = (f32[1,20,32,256]{3,2,1,0:T(8,128)S(1)}, f32[2,2,10,12,256]{4,3,2,1,0:T(8,128)S(1)}, bf16[1920,1024]{1,0:T(8,128)(2,1)S(1)}) custom-call(s32[2]{0:T(128)S(1)} %pad_add_fusion.place, bf16[640,1024]{1,0:T(8,128)(2,1)S(1)} %get-tuple-element.29.refs_0_, bf16[640,1024]{1,0:T(8,128)(2,1)S(1)} %collective-permute-done.refs_1_, ...), custom_call_target="tpu_custom_call" | custom-call | flops 125829120 | bytes 196608 | tf_op jit(solution)/shard_map/pallas_call | solution.py:383
  10.7 2.8 %collective-permute-start.1 = (f16[2,10,12,256]{3,2,1,0:T(8,128)(2,1)S(1)}, f16[2,10,12,256]{3,2,1,0:T(8,128)(2,1)S(1)}, u32[]{:S(2)}, u32[]{:S(2)}) collective-permute-start(f16[2,10,12,256]{3,2,1,0:T(8,128)(2,1)S(1)} %fusion.5), channel_id=1, source_target_pairs={{0,2},{2,0},{1,3},{3,1},{4,6},{6,4},{5,7},{7,5},{8,10},{10,8},{9,1... | collective-permute-start | bytes 368648 | tf_op jit(solution)/shard_map/ppermute | solution.py:335
  13.5 5.0 %shard_map.111 = (f32[2,20,32,256]{3,2,1,0:T(8,128)S(1)}, f32[2,2,10,24,256]{4,3,2,1,0:T(8,128)S(1)}) custom-call(s32[2]{0:T(128)S(1)} %pad_add_fusion.place, bf16[1920,1024]{1,0:T(8,128)(2,1)S(1)} %get-tuple-element.38.refs_0_.tall, bf16[3,3,3,1024,256]{4,3,2,1,0:T(8,128)(2,1)S(1)} %get-tuple-element.32.refs_2_.refs_1_.taps), custom_call_target="tpu_custom_call" | custom-call | flops 251658240 | bytes 393216 | tf_op jit(solution)/shard_map/pallas_call | solution.py:385
  18.6 3.8 %shard_map.112 = f32[2,320,1024]{2,1,0:T(8,128)S(1)} custom-call(s32[2]{0:T(128)S(1)} %pad_add_fusion.place, bf16[1920,1024]{1,0:T(8,128)(2,1)S(1)} %get-tuple-element.38.refs_0_.tall, bf16[3,3,3,1024,256]{4,3,2,1,0:T(8,128)(2,1)S(1)} %get-tuple-element.32.refs_2_.refs_1_.taps, f32[640,256]{1,0:T(8,128)S(1)} %get-tuple-element.30.point_sum, ...), custom_call_target="tpu_custom_call" | custom-call | flops 209715200 | bytes 327680 | tf_op jit(solution)/shard_map/pallas_call | solution.py:396
  23.4 1.4 %collective-permute-start.2 = (f16[320,1024]{1,0:T(8,128)(2,1)}, f16[320,1024]{1,0:T(8,128)(2,1)}, u32[]{:S(2)}, u32[]{:S(2)}) collective-permute-start(f16[320,1024]{1,0:T(8,128)(2,1)} %fusion.1), channel_id=1, source_target_pairs={{0,2},{2,0},{1,3},{3,1},{4,6},{6,4},{5,7},{7,5},{8,10},{10,8},{9,1... | collective-permute-start | bytes 1966088 | tf_op jit(solution)/shard_map/ppermute | solution.py:335
  25.9 1.3 %collective-permute-start.4 = (f16[10,24,256]{2,1,0:T(8,128)(2,1)S(1)}, f16[10,24,256]{2,1,0:T(8,128)(2,1)S(1)}, u32[]{:S(2)}, u32[]{:S(2)}) collective-permute-start(f16[10,24,256]{2,1,0:T(8,128)(2,1)S(1)} %get-tuple-element.54), channel_id=1, source_target_pairs={{0,4},{4,8},{8,12},{12,16},{16,20},{20,24},{24,28},{28,0},{1,5},{5... | collective-permute-start | bytes 368648 | tf_op jit(solution)/shard_map/ppermute | solution.py:341
  27.2 3.1 %collective-permute-start.5 = (f16[10,24,256]{2,1,0:T(8,128)(2,1)S(1)}, f16[10,24,256]{2,1,0:T(8,128)(2,1)S(1)}, u32[]{:S(2)}, u32[]{:S(2)}) collective-permute-start(f16[10,24,256]{2,1,0:T(8,128)(2,1)S(1)} %get-tuple-element.53), channel_id=1, source_target_pairs={{0,28},{4,0},{8,4},{12,8},{16,12},{20,16},{24,20},{28,24},{1,29},{... | collective-permute-start | bytes 368648 | tf_op jit(solution)/shard_map/ppermute | solution.py:338
  31.0 4.2 %collective-permute-start.7 = (f16[10,12,256]{2,1,0:T(8,128)(2,1)S(1)}, f16[10,12,256]{2,1,0:T(8,128)(2,1)S(1)}, u32[]{:S(2)}, u32[]{:S(2)}) collective-permute-start(f16[10,12,256]{2,1,0:T(8,128)(2,1)S(1)} %get-tuple-element.55), channel_id=1, source_target_pairs={{0,28},{4,0},{8,4},{12,8},{16,12},{20,16},{24,20},{28,24},{1,29},{... | collective-permute-start | bytes 184328 | tf_op jit(solution)/shard_map/ppermute | solution.py:338
  35.2 2.1 %collective-permute-done.6 = f16[10,12,256]{2,1,0:T(8,128)(2,1)S(1)} collective-permute-done((f16[10,12,256]{2,1,0:T(8,128)(2,1)}, f16[10,12,256]{2,1,0:T(8,128)(2,1)S(1)}, u32[]{:S(2)}, u32[]{:S(2)}) %collective-permute-start.6) | collective-permute-done | bytes 61472 | tf_op jit(solution)/shard_map/ppermute | solution.py:341
  37.5 2.7 %collective-permute-done.2 = f16[320,1024]{1,0:T(8,128)(2,1)} collective-permute-done((f16[320,1024]{1,0:T(8,128)(2,1)}, f16[320,1024]{1,0:T(8,128)(2,1)}, u32[]{:S(2)}, u32[]{:S(2)}) %collective-permute-start.2) | collective-permute-done | bytes 655392 | tf_op jit(solution)/shard_map/ppermute | solution.py:335
  40.2 1.3 %fusion.sums = f32[320,1024]{1,0:T(8,128)S(1)} fusion(f32[2,320,1024]{2,1,0:T(8,128)S(1)} %shard_map.112, f16[320,1024]{1,0:T(8,128)(2,1)} %collective-permute-done.2), kind=kLoop, calls=%fused_computation.2 | loop fusion | flops 655360 | bytes 3276800 | tf_op jit(solution)/shard_map/add | solution.py:414
  41.6 2.0 %shard_map.113 = (bf16[10,32,256]{2,1,0:T(8,128)(2,1)S(1)}, bf16[10,32,768]{2,1,0:T(8,128)(2,1)S(1)}, bf16[10,36,256]{2,1,0:T(8,128)(2,1)S(1)}, bf16[10,36,256]{2,1,0:T(8,128)(2,1)S(1)}) custom-call(s32[2]{0:T(128)S(1)} %pad_add_fusion.place, f32[320,1024]{1,0:T(8,128)S(1)} %fusion.sums, f32[10,24,256]{2,1,0:T(8,128)S(1)} %convert_element_type.50.left_a, ...), custom_call_target="tpu_custom_call" | custom-call | flops 23592960 | bytes 163840 | tf_op jit(solution)/shard_map/pallas_call | solution.py:420
  44.5 1.3 %collective-permute-start.12 = (bf16[10,32,768]{2,1,0:T(8,128)(2,1)S(1)}, bf16[10,32,768]{2,1,0:T(8,128)(2,1)S(1)}, u32[]{:S(2)}, u32[]{:S(2)}) collective-permute-start(bf16[10,32,768]{2,1,0:T(8,128)(2,1)S(1)} %get-tuple-element.45.own), channel_id=1, source_target_pairs={{0,2},{2,0},{1,3},{3,1},{4,6},{6,4},{5,7},{7,5},{8,10},{10,8},{9,1... | collective-permute-start | bytes 1474568 | tf_op jit(solution)/shard_map/ppermute | solution.py:335
  45.8 1.2 %collective-permute-start.8 = (bf16[10,36,256]{2,1,0:T(8,128)(2,1)S(1)}, bf16[10,36,256]{2,1,0:T(8,128)(2,1)S(1)}, u32[]{:S(2)}, u32[]{:S(2)}) collective-permute-start(bf16[10,36,256]{2,1,0:T(8,128)(2,1)S(1)} %get-tuple-element.44), channel_id=1, source_target_pairs={{0,4},{4,8},{8,12},{12,16},{16,20},{20,24},{24,28},{28,0},{1,5},{5... | collective-permute-start | bytes 552968 | tf_op jit(solution)/shard_map/ppermute | solution.py:341
  47.0 3.0 %collective-permute-start.10 = (bf16[10,36,256]{2,1,0:T(8,128)(2,1)S(1)}, bf16[10,36,256]{2,1,0:T(8,128)(2,1)S(1)}, u32[]{:S(2)}, u32[]{:S(2)}) collective-permute-start(bf16[10,36,256]{2,1,0:T(8,128)(2,1)S(1)} %get-tuple-element.48), channel_id=1, source_target_pairs={{0,28},{4,0},{8,4},{12,8},{16,12},{20,16},{24,20},{28,24},{1,29},{... | collective-permute-start | bytes 552968 | tf_op jit(solution)/shard_map/ppermute | solution.py:338
  50.1 8.4 %shard_map.114 = (f32[20,32,1024]{2,1,0:T(8,128)S(1)}, bf16[3,3,3,1024,256]{4,3,2,1,0:T(8,128)(2,1)S(1)}) custom-call(s32[2]{0:T(128)S(1)} %pad_add_fusion.place, bf16[10,32,768]{2,1,0:T(8,128)(2,1)S(1)} %get-tuple-element.45.own, bf16[10,32,768]{2,1,0:T(8,128)(2,1)S(1)} %collective-permute-done.9.other, bf16[3,3,3,1024,256]{4,3,2,1,0:T(8,128)(2,1)} %bitcast.38), custom_call_target="tpu_custom_call" | custom-call | flops 293601280 | bytes 458752 | tf_op jit(solution)/shard_map/pallas_call | solution.py:434
  58.6 1.8 %collective-permute-start.14 = (bf16[10,104,256]{2,1,0:T(8,128)(2,1)S(1)}, bf16[10,104,256]{2,1,0:T(8,128)(2,1)S(1)}, u32[]{:S(2)}, u32[]{:S(2)}) collective-permute-start(bf16[10,104,256]{2,1,0:T(8,128)(2,1)S(1)} %pad_maximum_fusion.own), channel_id=1, source_target_pairs={{0,1},{1,0},{2,3},{3,2},{4,5},{5,4},{6,7},{7,6},{8,9},{9,8},{10,11... | collective-permute-start | bytes 1597448 | tf_op jit(solution)/shard_map/ppermute | solution.py:332
  60.6 1.4 %collective-permute-done.14.other = bf16[10,104,256]{2,1,0:T(8,128)(2,1)S(1)} collective-permute-done((bf16[10,104,256]{2,1,0:T(8,128)(2,1)S(1)}, bf16[10,104,256]{2,1,0:T(8,128)(2,1)S(1)}, u32[]{:S(2)}, u32[]{:S(2)}) %collective-permute-start.14) | collective-permute-done | bytes 532512 | tf_op jit(solution)/shard_map/ppermute | solution.py:332
  62.0 4.6 %shard_map.115.refs_0_ = f32[20,32,1024]{2,1,0:T(8,128)S(1)} custom-call(s32[2]{0:T(128)S(1)} %pad_add_fusion.place, bf16[10,104,256]{2,1,0:T(8,128)(2,1)S(1)} %pad_maximum_fusion.own, bf16[10,104,256]{2,1,0:T(8,128)(2,1)S(1)} %collective-permute-done.14.other, bf16[3,3,3,1024,256]{4,3,2,1,0:T(8,128)(2,1)S(1)} %get-tuple-element.51.taps, ...), custom_call_target="tpu_custom_call" | custom-call | flops 104857600 | bytes 458752 | tf_op jit(solution)/shard_map/pallas_call | solution.py:441
  66.6 7.0 %shard_map.116.acc = f32[20,32,1024]{2,1,0:T(8,128)S(1)} custom-call(s32[2]{0:T(128)S(1)} %pad_add_fusion.place, bf16[10,32,768]{2,1,0:T(8,128)(2,1)S(1)} %collective-permute-done.12.own, bf16[10,32,768]{2,1,0:T(8,128)(2,1)S(1)} %collective-permute-done.13.other, bf16[3,3,3,1024,256]{4,3,2,1,0:T(8,128)(2,1)S(1)} %get-tuple-element.51.taps, ...), custom_call_target="tpu_custom_call" | custom-call | flops 293601280 | bytes 458752 | tf_op jit(solution)/shard_map/pallas_call | solution.py:456
  75.0 3.3 %shard_map.117.acc = f32[20,32,1024]{2,1,0:T(8,128)S(1)} custom-call(s32[2]{0:T(128)S(1)} %pad_add_fusion.place, bf16[10,104,256]{2,1,0:T(8,128)(2,1)S(1)} %collective-permute-done.11.own.other, bf16[10,104,256]{2,1,0:T(8,128)(2,1)S(1)} %collective-permute-done.11.own.other, bf16[3,3,3,1024,256]{4,3,2,1,0:T(8,128)(2,1)S(1)} %get-tuple-element.51.taps, ...), custom_call_target="tpu_custom_call" | custom-call | flops 104857600 | bytes 458752 | tf_op jit(solution)/shard_map/pallas_call | solution.py:441
  78.3 3.6 %shard_map.118 = bf16[20,32,1024]{2,1,0:T(8,128)(2,1)} custom-call(s32[2]{0:T(128)S(1)} %pad_add_fusion.place, bf16[10,104,256]{2,1,0:T(8,128)(2,1)S(1)} %collective-permute-done.11.own.other, bf16[10,104,256]{2,1,0:T(8,128)(2,1)S(1)} %collective-permute-done.15.other, bf16[3,3,3,1024,256]{4,3,2,1,0:T(8,128)(2,1)S(1)} %get-tuple-element.51.taps, ...), custom_call_target="tpu_custom_call" | custom-call | flops 104857600 | bytes 458752 | tf_op jit(solution)/shard_map/pallas_call | solution.py:441
  (61 shorter events, 6.8 us)
Async XLA Ops:
  0.0 7.7 %collective-permute-start = (bf16[640,1024]{1,0:T(8,128)(2,1)}, bf16[640,1024]{1,0:T(8,128)(2,1)S(1)}, u32[]{:S(2)}, u32[]{:S(2)}) collective-permute-start(bf16[640,1024]{1,0:T(8,128)(2,1)} %bitcast.33), channel_id=1, source_target_pairs={{0,1},{1,0},{2,3},{3,2},{4,5},{5,4},{6,7},{7,6},{8,9},{9,8},{10,11... | collective-permute-start | bytes 3932168 | tf_op jit(solution)/shard_map/ppermute | solution.py:332
  10.7 7.8 %collective-permute-start.1 = (f16[2,10,12,256]{3,2,1,0:T(8,128)(2,1)S(1)}, f16[2,10,12,256]{3,2,1,0:T(8,128)(2,1)S(1)}, u32[]{:S(2)}, u32[]{:S(2)}) collective-permute-start(f16[2,10,12,256]{3,2,1,0:T(8,128)(2,1)S(1)} %fusion.5), channel_id=1, source_target_pairs={{0,2},{2,0},{1,3},{3,1},{4,6},{6,4},{5,7},{7,5},{8,10},{10,8},{9,1... | collective-permute-start | bytes 368648 | tf_op jit(solution)/shard_map/ppermute | solution.py:335
  18.5 7.3 %collective-permute-start.3 = (f16[2,10,24,256]{3,2,1,0:T(8,128)(2,1)S(1)}, f16[2,10,24,256]{3,2,1,0:T(8,128)(2,1)S(1)}, u32[]{:S(2)}, u32[]{:S(2)}) collective-permute-start(f16[2,10,24,256]{3,2,1,0:T(8,128)(2,1)S(1)} %fusion.4), channel_id=1, source_target_pairs={{0,2},{2,0},{1,3},{3,1},{4,6},{6,4},{5,7},{7,5},{8,10},{10,8},{9,1... | collective-permute-start | bytes 737288 | tf_op jit(solution)/shard_map/ppermute | solution.py:335
  23.4 6.9 %copy-start.10 = (s32[1,1,5]{2,1,0:T(1,128)S(1)}, s32[1,1,5]{2,1,0:T(1,128)}, u32[]{:S(2)}) copy-start(s32[1,1,5]{2,1,0:T(1,128)} %param.13) | copy-start | bytes 64
  23.4 7.0 %copy-start.9 = (s32[20,32]{1,0:T(8,128)S(1)}, s32[20,32]{1,0:T(8,128)}, u32[]{:S(2)}) copy-start(s32[20,32]{1,0:T(8,128)} %param.12) | copy-start | bytes 7684
  23.4 16.7 %collective-permute-start.2 = (f16[320,1024]{1,0:T(8,128)(2,1)}, f16[320,1024]{1,0:T(8,128)(2,1)}, u32[]{:S(2)}, u32[]{:S(2)}) collective-permute-start(f16[320,1024]{1,0:T(8,128)(2,1)} %fusion.1), channel_id=1, source_target_pairs={{0,2},{2,0},{1,3},{3,1},{4,6},{6,4},{5,7},{7,5},{8,10},{10,8},{9,1... | collective-permute-start | bytes 1966088 | tf_op jit(solution)/shard_map/ppermute | solution.py:335
  25.9 11.4 %collective-permute-start.4 = (f16[10,24,256]{2,1,0:T(8,128)(2,1)S(1)}, f16[10,24,256]{2,1,0:T(8,128)(2,1)S(1)}, u32[]{:S(2)}, u32[]{:S(2)}) collective-permute-start(f16[10,24,256]{2,1,0:T(8,128)(2,1)S(1)} %get-tuple-element.54), channel_id=1, source_target_pairs={{0,4},{4,8},{8,12},{12,16},{16,20},{20,24},{24,28},{28,0},{1,5},{5... | collective-permute-start | bytes 368648 | tf_op jit(solution)/shard_map/ppermute | solution.py:341
  27.2 10.2 %collective-permute-start.5 = (f16[10,24,256]{2,1,0:T(8,128)(2,1)S(1)}, f16[10,24,256]{2,1,0:T(8,128)(2,1)S(1)}, u32[]{:S(2)}, u32[]{:S(2)}) collective-permute-start(f16[10,24,256]{2,1,0:T(8,128)(2,1)S(1)} %get-tuple-element.53), channel_id=1, source_target_pairs={{0,28},{4,0},{8,4},{12,8},{16,12},{20,16},{24,20},{28,24},{1,29},{... | collective-permute-start | bytes 368648 | tf_op jit(solution)/shard_map/ppermute | solution.py:338
  30.9 6.4 %collective-permute-start.6 = (f16[10,12,256]{2,1,0:T(8,128)(2,1)}, f16[10,12,256]{2,1,0:T(8,128)(2,1)S(1)}, u32[]{:S(2)}, u32[]{:S(2)}) collective-permute-start(f16[10,12,256]{2,1,0:T(8,128)(2,1)} %get-tuple-element.56), channel_id=1, source_target_pairs={{0,4},{4,8},{8,12},{12,16},{16,20},{20,24},{24,28},{28,0},{1,5},{5... | collective-permute-start | bytes 184328 | tf_op jit(solution)/shard_map/ppermute | solution.py:341
  31.0 6.3 %collective-permute-start.7 = (f16[10,12,256]{2,1,0:T(8,128)(2,1)S(1)}, f16[10,12,256]{2,1,0:T(8,128)(2,1)S(1)}, u32[]{:S(2)}, u32[]{:S(2)}) collective-permute-start(f16[10,12,256]{2,1,0:T(8,128)(2,1)S(1)} %get-tuple-element.55), channel_id=1, source_target_pairs={{0,28},{4,0},{8,4},{12,8},{16,12},{20,16},{24,20},{28,24},{1,29},{... | collective-permute-start | bytes 184328 | tf_op jit(solution)/shard_map/ppermute | solution.py:338
  37.4 4.1 %copy-start.3 = (bf16[1024,256]{1,0:T(8,128)(2,1)S(1)}, bf16[1024,256]{1,0:T(8,128)(2,1)}, u32[]{:S(2)}) copy-start(bf16[1024,256]{1,0:T(8,128)(2,1)} %w_proj.1) | copy-start | bytes 1572868
  37.4 4.1 %copy-start.4 = (bf16[256,128]{1,0:T(8,128)(2,1)S(1)}, bf16[256,128]{1,0:T(8,128)(2,1)}, u32[]{:S(2)}) copy-start(bf16[256,128]{1,0:T(8,128)(2,1)} %w_class.1) | copy-start | bytes 196612
  37.5 4.1 %copy-start.5 = (f32[4,256]{1,0:T(4,128)S(1)}, f32[4,256]{1,0:T(4,128)}, u32[]{:S(2)}) copy-start(f32[4,256]{1,0:T(4,128)} %scales.1) | copy-start | bytes 12292
  37.5 4.1 %copy-start.6 = (f32[4,256]{1,0:T(4,128)S(1)}, f32[4,256]{1,0:T(4,128)}, u32[]{:S(2)}) copy-start(f32[4,256]{1,0:T(4,128)} %shifts.1) | copy-start | bytes 12292
  37.5 4.1 %copy-start.7 = (f32[256]{0:T(256)S(1)}, f32[256]{0:T(256)}, u32[]{:S(2)}) copy-start(f32[256]{0:T(256)} %param.19) | copy-start | bytes 3076
  37.5 4.1 %copy-start.8 = (f32[256]{0:T(256)S(1)}, f32[256]{0:T(256)}, u32[]{:S(2)}) copy-start(f32[256]{0:T(256)} %param.20) | copy-start | bytes 3076
  43.6 6.5 %collective-permute-start.9 = (bf16[10,32,768]{2,1,0:T(8,128)(2,1)S(1)}, bf16[10,32,768]{2,1,0:T(8,128)(2,1)S(1)}, u32[]{:S(2)}, u32[]{:S(2)}) collective-permute-start(bf16[10,32,768]{2,1,0:T(8,128)(2,1)S(1)} %get-tuple-element.45.own), channel_id=1, source_target_pairs={{0,1},{1,0},{2,3},{3,2},{4,5},{5,4},{6,7},{7,6},{8,9},{9,8},{10,11... | collective-permute-start | bytes 1474568 | tf_op jit(solution)/shard_map/ppermute | solution.py:332
  44.5 15.9 %collective-permute-start.12 = (bf16[10,32,768]{2,1,0:T(8,128)(2,1)S(1)}, bf16[10,32,768]{2,1,0:T(8,128)(2,1)S(1)}, u32[]{:S(2)}, u32[]{:S(2)}) collective-permute-start(bf16[10,32,768]{2,1,0:T(8,128)(2,1)S(1)} %get-tuple-element.45.own), channel_id=1, source_target_pairs={{0,2},{2,0},{1,3},{3,1},{4,6},{6,4},{5,7},{7,5},{8,10},{10,8},{9,1... | collective-permute-start | bytes 1474568 | tf_op jit(solution)/shard_map/ppermute | solution.py:335
  45.8 12.7 %collective-permute-start.8 = (bf16[10,36,256]{2,1,0:T(8,128)(2,1)S(1)}, bf16[10,36,256]{2,1,0:T(8,128)(2,1)S(1)}, u32[]{:S(2)}, u32[]{:S(2)}) collective-permute-start(bf16[10,36,256]{2,1,0:T(8,128)(2,1)S(1)} %get-tuple-element.44), channel_id=1, source_target_pairs={{0,4},{4,8},{8,12},{12,16},{16,20},{20,24},{24,28},{28,0},{1,5},{5... | collective-permute-start | bytes 552968 | tf_op jit(solution)/shard_map/ppermute | solution.py:341
  47.0 11.5 %collective-permute-start.10 = (bf16[10,36,256]{2,1,0:T(8,128)(2,1)S(1)}, bf16[10,36,256]{2,1,0:T(8,128)(2,1)S(1)}, u32[]{:S(2)}, u32[]{:S(2)}) collective-permute-start(bf16[10,36,256]{2,1,0:T(8,128)(2,1)S(1)} %get-tuple-element.48), channel_id=1, source_target_pairs={{0,28},{4,0},{8,4},{12,8},{16,12},{20,16},{24,20},{28,24},{1,29},{... | collective-permute-start | bytes 552968 | tf_op jit(solution)/shard_map/ppermute | solution.py:338
  58.6 3.3 %collective-permute-start.14 = (bf16[10,104,256]{2,1,0:T(8,128)(2,1)S(1)}, bf16[10,104,256]{2,1,0:T(8,128)(2,1)S(1)}, u32[]{:S(2)}, u32[]{:S(2)}) collective-permute-start(bf16[10,104,256]{2,1,0:T(8,128)(2,1)S(1)} %pad_maximum_fusion.own), channel_id=1, source_target_pairs={{0,1},{1,0},{2,3},{3,2},{4,5},{5,4},{6,7},{7,6},{8,9},{9,8},{10,11... | collective-permute-start | bytes 1597448 | tf_op jit(solution)/shard_map/ppermute | solution.py:332
  60.4 13.7 %collective-permute-start.11 = (bf16[10,104,256]{2,1,0:T(8,128)(2,1)S(1)}, bf16[10,104,256]{2,1,0:T(8,128)(2,1)S(1)}, u32[]{:S(2)}, u32[]{:S(2)}) collective-permute-start(bf16[10,104,256]{2,1,0:T(8,128)(2,1)S(1)} %pad_maximum_fusion.own), channel_id=1, source_target_pairs={{0,2},{2,0},{1,3},{3,1},{4,6},{6,4},{5,7},{7,5},{8,10},{10,8},{9,1... | collective-permute-start | bytes 1597448 | tf_op jit(solution)/shard_map/ppermute | solution.py:335
  60.4 6.2 %collective-permute-start.13 = (bf16[10,32,768]{2,1,0:T(8,128)(2,1)S(1)}, bf16[10,32,768]{2,1,0:T(8,128)(2,1)S(1)}, u32[]{:S(2)}, u32[]{:S(2)}) collective-permute-start(bf16[10,32,768]{2,1,0:T(8,128)(2,1)S(1)} %collective-permute-done.12.own), channel_id=1, source_target_pairs={{0,1},{1,0},{2,3},{3,2},{4,5},{5,4},{6,7},{7,6},{8,9},{9,8},{10,11... | collective-permute-start | bytes 1474568 | tf_op jit(solution)/shard_map/ppermute | solution.py:332
  74.1 4.2 %collective-permute-start.15 = (bf16[10,104,256]{2,1,0:T(8,128)(2,1)S(1)}, bf16[10,104,256]{2,1,0:T(8,128)(2,1)S(1)}, u32[]{:S(2)}, u32[]{:S(2)}) collective-permute-start(bf16[10,104,256]{2,1,0:T(8,128)(2,1)S(1)} %collective-permute-done.11.own.other), channel_id=1, source_target_pairs={{0,1},{1,0},{2,3},{3,2},{4,5},{5,4},{6,7},{7,6},{8,9},{9,8},{10,11... | collective-permute-start | bytes 1597448 | tf_op jit(solution)/shard_map/ppermute | solution.py:332
  (3 other events, 5.8 us)
